TPU v7x, 128 devices: a whole 4x4x4 slice. The times are simulated.
128 devices in a mesh: dp: 16 (over y_lo, x, core), tensor: 8 (over y_hi, z).
Axes of the slice: x: 4, y: 4 (y_hi: 2, y_lo: 2; y = y_hi * 2 + y_lo), z: 4, core: 2. Of those that a mesh axis runs over, the one named last changes fastest.
Arguments:
- block_input: bfloat16 [16, 1024, 1024], P('dp', 'tensor'), may hold values from -6 to 6
- mixer_gain: float32 [1, 1024], replicated, may hold values from 0.25 to 1.75
- query_key_weight: bfloat16 [1, 1024, 8, 256], P(None, 'dp', 'tensor'), may hold values from -0.1875 to 0.1875
- value_gate_weight: bfloat16 [1, 1024, 8, 512], P(None, 'dp', 'tensor'), may hold values from -0.1875 to 0.1875
- beta_decay_weight: bfloat16 [1, 1024, 8, 2], P(None, 'dp', 'tensor'), may hold values from -0.1875 to 0.1875
- conv_query_key: float32 [1, 4, 8, 256], P(None, None, 'tensor'), may hold values from -3 to 3
- conv_value: float32 [1, 4, 8, 256], P(None, None, 'tensor'), may hold values from -3 to 3
- decay_log: float32 [1, 8], P(None, 'tensor'), may hold values from 0 to 0.7
- decay_bias: float32 [1, 8], P(None, 'tensor'), may hold values from -6.9 to -4.2
- out_gain: float32 [1, 256], replicated, may hold values from 0.25 to 1.75
- out_weight: bfloat16 [1, 8, 256, 1024], P(None, 'tensor', None, 'dp'), may hold values from -0.25 to 0.25
- forward_gain: float32 [1, 1024], replicated, may hold values from 0.25 to 1.75
- gate_up_weight: bfloat16 [1, 1024, 2, 2816], P(None, 'dp', None, 'tensor'), may hold values from -0.1875 to 0.1875
- down_weight: bfloat16 [1, 2816, 1024], P(None, 'tensor', 'dp'), may hold values from -0.21875 to 0.21875
- out_cotangent: bfloat16 [16, 1024, 1024], P('dp', 'tensor'), may hold values from -6 to 6
Outputs:
- block_output: float32 [16, 1024, 1024], P('dp', 'tensor')
- input_grad: float32 [16, 1024, 1024], P('dp', 'tensor')
- grad_mixer_gain: float32 [1, 1024], replicated
- grad_query_key: float32 [1, 1024, 8, 256], P(None, 'dp', 'tensor')
- grad_value_gate: float32 [1, 1024, 8, 512], P(None, 'dp', 'tensor')
- grad_beta_decay: float32 [1, 1024, 8, 2], P(None, 'dp', 'tensor')
- grad_conv_query_key: float32 [1, 4, 8, 256], P(None, None, 'tensor')
- grad_conv_value: float32 [1, 4, 8, 256], P(None, None, 'tensor')
- grad_decay_log: float32 [1, 8], P(None, 'tensor')
- grad_decay_bias: float32 [1, 8], P(None, 'tensor')
- grad_out_gain: float32 [1, 256], replicated
- grad_out_weight: float32 [1, 8, 256, 1024], P(None, 'tensor', None, 'dp')
- grad_forward_gain: float32 [1, 1024], replicated
- gradient_gate_up_weight: float32 [1, 1024, 2, 2816], P(None, 'dp', None, 'tensor')
- grad_down: float32 [1, 2816, 1024], P(None, 'tensor', 'dp')
All inputs are finite; a program needn't handle non-finite values.
Results may differ from a plain program's by a relative error of at most 0.02.
Values may be sent and summed in bfloat16 or wider, within the bound.
A program may use at most 128 MiB of HBM per device.

v0:
```python
import jax
import jax.numpy as jnp
from jax import lax
from jax.sharding import PartitionSpec as P

SPAN = 64


EPS = 1e-06
GATED_EPS = 1e-05
PRECISE = lax.Precision.HIGHEST


def sent_to_all(x, axis):
    copies = jnp.broadcast_to(x, (lax.axis_size(axis), *x.shape))
    return lax.all_to_all(copies, axis, split_axis=0, concat_axis=0, tiled=True)


def laid_out(tiles, dim):
    tiles = jnp.moveaxis(tiles, 0, dim)
    shape = tiles.shape
    return tiles.reshape(*shape[:dim], shape[dim] * shape[dim + 1], *shape[dim + 2 :])


def collect_2(x, axis, dim):
    tiles = sent_to_all(x, axis)
    return laid_out(tiles, dim)


def split_up(x, dim, size):
    before, after = (x.shape[:dim], x.shape[dim + 1 :])
    return jnp.moveaxis(x.reshape(*before, size, -1, *after), dim, 0)


def summed_on_arrival(x, axis, dim):
    size = lax.axis_size(axis)
    tiles = lax.all_to_all(split_up(x, dim, size), axis, 0, 0, tiled=True)
    return jnp.sum(tiles, axis=0)


def packed_total(arrays, axis):
    vector, at, finished = (jnp.concatenate([a.reshape(-1) for a in arrays]), 0, [])
    so_far = lax.psum(vector, axis)
    for a in arrays:
        finished.append(so_far[at : at + a.size].reshape(a.shape))
        at += a.size
    return tuple(finished)


def norm_rows(values, gain, offset=EPS):
    return values * lax.rsqrt(jnp.mean(values * values, -1, keepdims=True) + offset) * gain


def causal_conv(inputs, taps):
    length = inputs.shape[0]
    padded = jnp.pad(inputs, ((taps.shape[0] - 1, 0), (0, 0), (0, 0)))
    summed = padded[0:length] * taps[0]
    for shift_at in range(1, taps.shape[0]):
        summed = summed + padded[shift_at : shift_at + length] * taps[shift_at]
    return summed


def span_step(memory, block):
    queries, keys_in, values_in, beta_rows, log_decay = block
    block_len = log_decay.shape[0]
    cumulative = jnp.cumsum(log_decay)
    row_index = lax.broadcasted_iota(jnp.int32, (block_len, block_len), 0)
    col_index = lax.broadcasted_iota(jnp.int32, (block_len, block_len), 1)
    lower_eq = (row_index >= col_index).astype(jnp.float32)
    strict_lower = (row_index > col_index).astype(jnp.float32)
    decay_table = (
        jnp.exp(jnp.where(row_index >= col_index, cumulative[:, None] - cumulative[None, :], 0.0))
        * lower_eq
    )
    scale_in = jnp.exp(cumulative)
    key_inner = jnp.dot(keys_in, keys_in.T, precision=PRECISE)
    system = (
        jnp.eye(block_len, dtype=jnp.float32)
        + beta_rows[:, None] * key_inner * decay_table * strict_lower
    )
    right_side = beta_rows[:, None] * (
        values_in - scale_in[:, None] * jnp.dot(keys_in, memory, precision=PRECISE)
    )
    updates = jax.scipy.linalg.solve_triangular(system, right_side, lower=True, unit_diagonal=True)
    scores = jnp.dot(queries, keys_in.T, precision=PRECISE) * decay_table
    output = scale_in[:, None] * jnp.dot(queries, memory, precision=PRECISE) + jnp.dot(
        scores, updates, precision=PRECISE
    )
    tail_decay = jnp.exp(cumulative[-1] - cumulative)
    new_memory = jnp.exp(cumulative[-1]) * memory + jnp.dot(
        (keys_in * tail_decay[:, None]).T, updates, precision=PRECISE
    )
    return (new_memory, output)


def delta_head(queries, keys_in, values_in, beta_rows, log_decay):
    length = queries.shape[0]
    blocks = (
        queries.reshape(-1, SPAN, queries.shape[-1]),
        keys_in.reshape(-1, SPAN, keys_in.shape[-1]),
        values_in.reshape(-1, SPAN, values_in.shape[-1]),
        beta_rows.reshape(-1, SPAN),
        log_decay.reshape(-1, SPAN),
    )
    start = jnp.zeros((queries.shape[-1], values_in.shape[-1]), jnp.float32)
    final_memory, outputs = lax.scan(jax.checkpoint(span_step), start, blocks)
    return outputs.reshape(length, values_in.shape[-1])


def mixer_core(
    query_key_pre,
    value_gate_pre,
    beta_decay_pre,
    conv_query_key,
    conv_value,
    decay_log,
    decay_bias,
    out_gain,
):
    head_dim = query_key_pre.shape[-1] // 2
    value_dim = value_gate_pre.shape[-1] // 2
    conv_rows = jax.nn.silu(causal_conv(query_key_pre, conv_query_key))
    queries = conv_rows[..., :head_dim]
    keys_in = conv_rows[..., head_dim:]
    queries = (
        queries
        * lax.rsqrt(jnp.sum(queries * queries, -1, keepdims=True) + EPS)
        * head_dim ** (-0.5)
    )
    keys_in = keys_in * lax.rsqrt(jnp.sum(keys_in * keys_in, -1, keepdims=True) + EPS)
    values_in = jax.nn.silu(causal_conv(value_gate_pre[..., :value_dim], conv_value))
    gates = value_gate_pre[..., value_dim:]
    beta_rows = jax.nn.sigmoid(beta_decay_pre[..., 0])
    log_decay = -jnp.exp(decay_log) * jax.nn.softplus(beta_decay_pre[..., 1] + decay_bias)
    delta_out = jax.vmap(delta_head, in_axes=1, out_axes=1)(
        queries, keys_in, values_in, beta_rows, log_decay
    )
    return norm_rows(delta_out, out_gain, GATED_EPS) * jax.nn.silu(gates)


def spread(rows_low):
    return collect_2(rows_low, "tensor", 1)


def collect(terms):
    return summed_on_arrival(terms, "tensor", 1)


def collect_grad(terms):
    return summed_on_arrival(terms, "tensor", 1)


def body(
    block_input,
    mixer_gain,
    query_key_weight,
    value_gate_weight,
    beta_decay_weight,
    conv_query_key,
    conv_value,
    decay_log,
    decay_bias,
    out_gain,
    out_weight,
    forward_gain,
    gate_up_weight,
    down_weight,
    out_cotangent,
):
    layer_count = query_key_weight.shape[0]
    core_batch = jax.vmap(mixer_core, in_axes=(0, 0, 0, None, None, None, None, None))
    stream = block_input.astype(jnp.float32)
    layer_num = 0
    fetched = (
        lax.all_gather(query_key_weight[layer_num], "dp", axis=0, tiled=True),
        lax.all_gather(value_gate_weight[layer_num], "dp", axis=0, tiled=True),
        lax.all_gather(beta_decay_weight[layer_num], "dp", axis=0, tiled=True),
        lax.all_gather(out_weight[layer_num], "dp", axis=2, tiled=True),
        lax.all_gather(gate_up_weight[layer_num], "dp", axis=0, tiled=True),
        lax.all_gather(down_weight[layer_num], "dp", axis=1, tiled=True),
    )
    (
        query_key_projection,
        value_gate_projection,
        beta_decay_projection,
        output_projection_rows,
        gate_up_projection,
        down_projection_output,
    ) = fetched
    before_mixer = stream
    mixer_branch_rows = spread(norm_rows(stream, mixer_gain[layer_num]).astype(jnp.bfloat16))
    query_key_pre = jnp.einsum(
        "ebg,gwp->ebwp", mixer_branch_rows, query_key_projection, preferred_element_type=jnp.float32
    )
    value_gate_pre = jnp.einsum(
        "ebg,gwp->ebwp",
        mixer_branch_rows,
        value_gate_projection,
        preferred_element_type=jnp.float32,
    )
    beta_decay_pre = jnp.einsum(
        "ebg,gwp->ebwp",
        mixer_branch_rows,
        beta_decay_projection,
        preferred_element_type=jnp.float32,
    )
    mixed, core_back = jax.vjp(
        core_batch,
        query_key_pre,
        value_gate_pre,
        beta_decay_pre,
        conv_query_key[layer_num],
        conv_value[layer_num],
        decay_log[layer_num],
        decay_bias[layer_num],
        out_gain[layer_num],
    )
    mixed_reduced_precision = mixed.astype(jnp.bfloat16)
    stream = stream + collect(
        jnp.einsum(
            "kauj,ujx->kax",
            mixed_reduced_precision,
            output_projection_rows,
            preferred_element_type=jnp.float32,
        )
    )
    before_forward = stream
    forward_branch_rows = spread(norm_rows(stream, forward_gain[layer_num]).astype(jnp.bfloat16))
    gate_up = jnp.einsum(
        "enj,jzx->enzx", forward_branch_rows, gate_up_projection, preferred_element_type=jnp.float32
    )
    hidden_activation = (jax.nn.silu(gate_up[:, :, 0]) * gate_up[:, :, 1]).astype(jnp.bfloat16)
    stream = stream + collect(
        jnp.einsum(
            "htm,mx->htx",
            hidden_activation,
            down_projection_output,
            preferred_element_type=jnp.float32,
        )
    )
    saved = [
        (
            fetched,
            before_mixer,
            mixer_branch_rows,
            core_back,
            mixed_reduced_precision,
            before_forward,
            forward_branch_rows,
            gate_up,
            hidden_activation,
        )
    ]
    grad_stream = out_cotangent.astype(jnp.float32)
    weight_lists = [[], [], [], [], [], []]
    gain_lists = [[], [], []]
    head_lists = [[], [], [], []]
    for layer_num in reversed(range(layer_count)):
        (
            fetched,
            before_mixer,
            mixer_branch_rows,
            core_back,
            mixed_reduced_precision,
            before_forward,
            forward_branch_rows,
            gate_up,
            hidden_activation,
        ) = saved[layer_num]
        (
            query_key_projection,
            value_gate_projection,
            beta_decay_projection,
            output_projection_rows,
            gate_up_projection,
            down_projection_output,
        ) = fetched
        gradient_row_block = spread(grad_stream.astype(jnp.bfloat16))
        grad_hidden = jnp.einsum(
            "aok,ek->aoe",
            gradient_row_block,
            down_projection_output,
            preferred_element_type=jnp.float32,
        )
        grad_down_layer = jnp.einsum(
            "arq,ari->qi", hidden_activation, gradient_row_block, preferred_element_type=jnp.float32
        )
        gate_pre = gate_up[:, :, 0]
        up_pre = gate_up[:, :, 1]
        sigma = jax.nn.sigmoid(gate_pre)
        grad_gate = grad_hidden * up_pre * sigma * (1.0 + gate_pre * (1.0 - sigma))
        grad_up = grad_hidden * gate_pre * sigma
        gradient_gate_up_weight = jnp.stack([grad_gate, grad_up], 2).astype(jnp.bfloat16)
        grad_gu_layer = jnp.einsum(
            "hgp,hgjq->pjq",
            forward_branch_rows,
            gradient_gate_up_weight,
            preferred_element_type=jnp.float32,
        )
        grad_normed = collect_grad(
            jnp.einsum(
                "eiht,xht->eix",
                gradient_gate_up_weight,
                gate_up_projection,
                preferred_element_type=jnp.float32,
            )
        )
        unused_rows, norm_back = jax.vjp(norm_rows, before_forward, forward_gain[layer_num])
        grad_before, grad_fgain = norm_back(grad_normed)
        grad_stream = grad_stream + grad_before
        gradient_row_block = spread(grad_stream.astype(jnp.bfloat16))
        grad_mixed = jnp.einsum(
            "njk,eik->njei",
            gradient_row_block,
            output_projection_rows,
            preferred_element_type=jnp.float32,
        )
        grad_out_layer = jnp.einsum(
            "pvkq,pvi->kqi",
            mixed_reduced_precision,
            gradient_row_block,
            preferred_element_type=jnp.float32,
        )
        (
            gradient_query_key_input,
            gradient_value_gate_input,
            gradient_beta_decay_input,
            grad_cqk,
            grad_cv,
            grad_dlog,
            grad_dbias,
            grad_ogain,
        ) = core_back(grad_mixed)
        gradient_query_key_input = gradient_query_key_input.astype(jnp.bfloat16)
        gradient_value_gate_input = gradient_value_gate_input.astype(jnp.bfloat16)
        gradient_beta_decay_input = gradient_beta_decay_input.astype(jnp.bfloat16)
        grad_qk_layer = jnp.einsum(
            "zxv,zxrp->vrp",
            mixer_branch_rows,
            gradient_query_key_input,
            preferred_element_type=jnp.float32,
        )
        grad_vg_layer = jnp.einsum(
            "zxv,zxrp->vrp",
            mixer_branch_rows,
            gradient_value_gate_input,
            preferred_element_type=jnp.float32,
        )
        grad_bd_layer = jnp.einsum(
            "zxv,zxrp->vrp",
            mixer_branch_rows,
            gradient_beta_decay_input,
            preferred_element_type=jnp.float32,
        )
        row_terms = jnp.einsum(
            "piqb,vqb->piv",
            gradient_query_key_input,
            query_key_projection,
            preferred_element_type=jnp.float32,
        )
        row_terms = row_terms + jnp.einsum(
            "piqb,vqb->piv",
            gradient_value_gate_input,
            value_gate_projection,
            preferred_element_type=jnp.float32,
        )
        row_terms = row_terms + jnp.einsum(
            "piqb,vqb->piv",
            gradient_beta_decay_input,
            beta_decay_projection,
            preferred_element_type=jnp.float32,
        )
        grad_normed = collect_grad(row_terms)
        unused_rows, norm_back = jax.vjp(norm_rows, before_mixer, mixer_gain[layer_num])
        grad_before, grad_mgain = norm_back(grad_normed)
        grad_stream = grad_stream + grad_before
        owned = (
            grad_qk_layer,
            grad_vg_layer,
            grad_bd_layer,
            grad_out_layer,
            grad_gu_layer,
            grad_down_layer,
        )
        for slot_num in range(6):
            weight_lists[slot_num].insert(0, owned[slot_num])
        gain_lists[0].insert(0, grad_mgain)
        gain_lists[1].insert(0, grad_fgain)
        gain_lists[2].insert(0, grad_ogain)
        head_lists[0].insert(0, grad_cqk)
        head_lists[1].insert(0, grad_cv)
        head_lists[2].insert(0, grad_dlog)
        head_lists[3].insert(0, grad_dbias)
    stacked = [jnp.stack(weight_lists[slot_num]) for slot_num in range(6)]
    stacked = (
        lax.psum_scatter(
            stacked[0].astype(jnp.bfloat16), "dp", scatter_dimension=1, tiled=True
        ).astype(jnp.float32),
        lax.psum_scatter(
            stacked[1].astype(jnp.bfloat16), "dp", scatter_dimension=1, tiled=True
        ).astype(jnp.float32),
        lax.psum_scatter(
            stacked[2].astype(jnp.bfloat16), "dp", scatter_dimension=1, tiled=True
        ).astype(jnp.float32),
        lax.psum_scatter(
            stacked[3].astype(jnp.bfloat16), "dp", scatter_dimension=3, tiled=True
        ).astype(jnp.float32),
        lax.psum_scatter(
            stacked[4].astype(jnp.bfloat16), "dp", scatter_dimension=1, tiled=True
        ).astype(jnp.float32),
        lax.psum_scatter(
            stacked[5].astype(jnp.bfloat16), "dp", scatter_dimension=2, tiled=True
        ).astype(jnp.float32),
    )
    gain_totals = packed_total(
        (jnp.stack(gain_lists[0]), jnp.stack(gain_lists[1]), jnp.stack(gain_lists[2])),
        ("dp", "tensor"),
    )
    head_totals = lax.psum(
        (
            jnp.stack(head_lists[0]),
            jnp.stack(head_lists[1]),
            jnp.stack(head_lists[2]),
            jnp.stack(head_lists[3]),
        ),
        "dp",
    )
    return (
        stream,
        grad_stream,
        gain_totals[0],
        stacked[0],
        stacked[1],
        stacked[2],
        head_totals[0],
        head_totals[1],
        head_totals[2],
        head_totals[3],
        gain_totals[2],
        stacked[3],
        gain_totals[1],
        stacked[4],
        stacked[5],
    )


def solution(mesh):
    placed = (
        P("dp", "tensor", None),
        P(),
        P(None, "dp", "tensor", None),
        P(None, "dp", "tensor", None),
        P(None, "dp", "tensor", None),
        P(None, None, "tensor", None),
        P(None, None, "tensor", None),
        P(None, "tensor"),
        P(None, "tensor"),
        P(),
        P(None, "tensor", None, "dp"),
        P(),
        P(None, "dp", None, "tensor"),
        P(None, "tensor", "dp"),
        P("dp", "tensor", None),
    )
    return jax.shard_map(
        body,
        mesh=mesh,
        in_specs=placed,
        out_specs=(
            P("dp", "tensor", None),
            P("dp", "tensor", None),
            P(),
            P(None, "dp", "tensor", None),
            P(None, "dp", "tensor", None),
            P(None, "dp", "tensor", None),
            P(None, None, "tensor", None),
            P(None, None, "tensor", None),
            P(None, "tensor"),
            P(None, "tensor"),
            P(),
            P(None, "tensor", None, "dp"),
            P(),
            P(None, "dp", None, "tensor"),
            P(None, "tensor", "dp"),
        ),
        check_vma=False,
    )
```

profile of v0, /device:TPU:1, one launch (start us, length us, event | category | flops | bytes accessed | tf_op | source)
XLA Modules:
  0.0 1322.9 jit_solution(12888509850970778566)
XLA Ops:
  11.5 8.6 all-to-all-start
  21.1 21.4 %all-gather = bf16[1,1024,1,2]{3,2,0,1:T(2,128)(2,1)S(1)} all-gather(bf16[1,64,1,2]{3,2,0,1:T(2,128)(2,1)S(1)} %copy.106), channel_id=2, replica_groups=mesh['dp'=16,'tensor'=8] {'dp'}, dimensions={1}, use_global_device_ids=true | all-gather | bytes 4352 | tf_op jit(solution)/shard_map/all_gather | solution.py:177
  44.3 17.7 %all-gather.1 = bf16[1,1024,1,256]{3,1,2,0:T(8,128)(2,1)S(1)} all-gather(bf16[1,64,1,256]{3,1,2,0:T(8,128)(2,1)S(1)} %copy-done.44), channel_id=3, replica_groups=mesh['dp'=16,'tensor'=8] {'dp'}, dimensions={1}, use_global_device_ids=true | all-gather | bytes 557056 | tf_op jit(solution)/shard_map/all_gather | solution.py:175
  62.0 20.4 %all-gather.3 = bf16[1,1,256,1024]{2,3,1,0:T(8,128)(2,1)} all-gather(bf16[1,1,256,64]{2,3,1,0:T(8,128)(2,1)S(1)} %copy-done.45), channel_id=5, replica_groups=mesh['dp'=16,'tensor'=8] {'dp'}, dimensions={3}, use_global_device_ids=true | all-gather | bytes 557056 | tf_op jit(solution)/shard_map/all_gather | solution.py:178
  95.4 215.0 %while.41 = (s32[]{:T(128)}, f32[1,1,128,256]{3,2,1,0:T(8,128)S(1)}, f32[16,1,1,64,256]{4,3,2,1,0:T(8,128)S(1)}, f32[16,1,1,128,256]{4,3,2,1,0:T(8,128)}, f32[16...) while((s32[]{:T(128)}, ...), condition=%wide.region_5.7_spmd.clone, body=%wide.region_3.6_spmd.clone.sunk | while | flops 113635392 | bytes 1666214 | solution.py:106
  98.9 4.9 custom-call.26
  112.4 4.9 custom-call.26
  125.8 4.9 custom-call.26
  139.2 4.9 custom-call.26
  152.7 4.9 custom-call.26
  166.1 4.9 custom-call.26
  179.6 4.9 custom-call.26
  193.0 4.9 custom-call.26
  206.5 4.9 custom-call.26
  219.9 4.9 custom-call.26
  233.3 4.9 custom-call.26
  246.8 4.9 custom-call.26
  260.2 4.9 custom-call.26
  273.7 4.9 custom-call.26
  287.1 4.9 custom-call.26
  300.5 4.9 custom-call.26
  313.2 57.0 %all_to_all.40 = f32[8,1,128,1024]{3,2,1,0:T(8,128)} all-to-all(f32[8,1,128,1024]{3,2,1,0:T(8,128)S(1)} %convolution_bitcast_fusion.11), channel_id=1, replica_groups=mesh['dp'=16,'tensor'=8] {'tensor'}, dimensions={0} | all-to-all | bytes 8388608 | tf_op jit(solution)/shard_map/all_to_all | solution.py:37
  380.1 27.7 %all-to-all-done.2 = bf16[8,1,128,1024]{3,2,1,0:T(8,128)(2,1)} async-done(((bf16[8,1,128,1024]{3,2,1,0:T(8,128)(2,1)}), bf16[8,1,128,1024]{3,2,1,0:T(8,128)(2,1)}, u32[]{:S(2)}, u32[]{:S(2)}) %all-to-all-start.2) | async-done | bytes 2097184 | tf_op jit(solution)/shard_map/all_to_all | solution.py:16
  413.8 24.8 %all-gather.5 = bf16[1,352,1024]{1,2,0:T(8,128)(2,1)} all-gather(bf16[1,352,64]{1,2,0:T(8,128)(2,1)S(1)} %copy-done.36), channel_id=7, replica_groups=mesh['dp'=16,'tensor'=8] {'dp'}, dimensions={2}, use_global_device_ids=true | all-gather | bytes 765952 | tf_op jit(solution)/shard_map/all_gather | solution.py:180
  438.6 4.9 copy.120
  443.5 5.3 convolution_bitcast_fusion.12
  458.5 6.8 all-to-all-start.5
  476.9 39.1 %all-to-all-done.5 = f32[8,1,128,1024]{3,2,1,0:T(8,128)} async-done(((f32[8,1,128,1024]{3,2,1,0:T(8,128)}), f32[8,1,128,1024]{3,2,1,0:T(8,128)}, u32[]{:S(2)}, u32[]{:S(2)}) %all-to-all-start.5) | async-done | bytes 4194336 | tf_op jit(solution)/shard_map/all_to_all | solution.py:37
  531.3 5.0 copy.138
  541.1 5.6 convolution_bitcast_fusion.10
  546.7 5.9 all-to-all-done.6
  552.6 5.2 all-to-all-start.3
  565.6 422.0 %while.42 = (s32[]{:T(128)}, f32[1,1,128,256]{2,3,1,0:T(8,128)S(1)}, f32[16,1,1,64,128]{4,3,2,1,0:T(8,128)S(1)}, f32[16,1,1,64,128]{4,3,2,1,0:T(8,128)S(1)}, f32...) while((s32[]{:T(128)}, ...), condition=%wide.region_25.27_spmd.clone, body=%wide.region_13.26_spmd.clone.sunk | while | flops 306119104 | bytes 5687583 | solution.py:106
  569.5 4.9 custom-call.28
  575.0 4.9 custom-call.27
  595.9 4.9 custom-call.28
  601.4 4.9 custom-call.27
  622.3 4.9 custom-call.28
  627.8 4.9 custom-call.27
  648.7 4.9 custom-call.28
  654.1 4.9 custom-call.27
  675.0 4.9 custom-call.28
  680.5 4.9 custom-call.27
  701.4 4.9 custom-call.28
  706.9 4.9 custom-call.27
  727.8 4.9 custom-call.28
  733.3 4.9 custom-call.27
  754.2 4.9 custom-call.28
  759.6 4.9 custom-call.27
  780.5 4.9 custom-call.28
  786.0 4.9 custom-call.27
  806.9 4.9 custom-call.28
  812.4 4.9 custom-call.27
  833.3 4.9 custom-call.28
  859.7 4.9 custom-call.28
  891.5 4.9 custom-call.27
  944.3 4.9 custom-call.27
  970.7 4.9 custom-call.27
  1012.5 6.7 all-to-all-start.7
  1033.5 32.0 %all-reduce.27 = (f32[1,4,1,256]{3,2,1,0:T(1,128)}, f32[1,4,1,256]{3,2,1,0:T(1,128)}, f32[1,1]{1,0:T(1,128)}, f32[1,1]{1,0:T(1,128)}) all-reduce(f32[1,4,1,256]{3,2,1,0:T(1,128)S(1)} %add_bitcast_fusion.2, f32[1,4,1,256]{3,2,1,0:T(1,128)S(1)} %add_bitcast_fusion.1, f32[1,1]{1,0:T(1,128)} %bitcast.98, ...), channel_id=1, replica_groups=mesh['dp'=16,'tensor'=8] {'dp'}, use_global_device_ids=true, to_apply=%region_41.43 | all-reduce | flops 2050 | bytes 16400 | tf_op jit(solution)/shard_map/psum | solution.py:419
  1066.9 48.8 %reduce-scatter.18.cloned.1.call-done = bf16[64,256]{1,0:T(8,128)(2,1)} async-done(((bf16[1024,256]{1,0:T(8,128)(2,1)}), bf16[64,256]{1,0:T(8,128)(2,1)}) %reduce-scatter.18.cloned.1.call-update) | async-done | bytes 32784
  1117.3 60.4 %reduce-scatter.12.cloned.1.call-done = bf16[1,64,1,256]{3,1,2,0:T(8,128)(2,1)} async-done(((bf16[1,1024,1,256]{3,1,2,0:T(8,128)(2,1)}), bf16[1,64,1,256]{3,1,2,0:T(8,128)(2,1)}) %reduce-scatter.12.cloned.1.call-update) | async-done | bytes 32784 | tf_op jit(solution)/shard_map/reduce_scatter | solution.py:396
  1179.1 60.8 %reduce-scatter.14.cloned.1.call-done = bf16[1,64,1,512]{3,1,2,0:T(8,128)(2,1)} async-done(((bf16[1,1024,1,512]{3,1,2,0:T(8,128)(2,1)}), bf16[1,64,1,512]{3,1,2,0:T(8,128)(2,1)}) %reduce-scatter.14.cloned.1.call-update) | async-done | bytes 65552 | tf_op jit(solution)/shard_map/reduce_scatter | solution.py:399
  1244.6 68.6 %psum.35 = f32[2304]{0:T(1024)S(1)} all-reduce(f32[2304]{0:T(1024)S(1)} %pad_maximum_fusion), channel_id=1, replica_groups=mesh['dp'=16,'tensor'=8] {'dp','tensor'}, use_global_device_ids=true, to_apply=%region_33.35 | all-reduce | flops 2304 | bytes 18432 | tf_op jit(solution)/shard_map/psum | solution.py:43
  (1193 shorter events, 534.1 us)
Async XLA Ops:
  11.5 9.4 copy-start.78
  11.5 32.6 %copy-start.73 = (f32[1,4,1,256]{3,2,1,0:T(1,128)S(1)}, f32[1,4,1,256]{3,2,1,0:T(1,128)}, u32[]{:S(2)}) copy-start(f32[1,4,1,256]{3,2,1,0:T(1,128)} %param.26) | copy-start | bytes 12292
  11.5 32.6 %copy-start.74 = (f32[1,4,1,256]{3,2,1,0:T(1,128)S(1)}, f32[1,4,1,256]{3,2,1,0:T(1,128)}, u32[]{:S(2)}) copy-start(f32[1,4,1,256]{3,2,1,0:T(1,128)} %param.27) | copy-start | bytes 12292
  11.5 32.7 %copy-start.44 = (bf16[1,64,1,256]{3,1,2,0:T(8,128)(2,1)S(1)}, bf16[1,64,1,256]{3,1,2,0:T(8,128)(2,1)}, u32[]{:S(2)}) copy-start(bf16[1,64,1,256]{3,1,2,0:T(8,128)(2,1)} %param.23) | copy-start | bytes 98308
  11.5 50.5 %copy-start.45 = (bf16[1,1,256,64]{2,3,1,0:T(8,128)(2,1)S(1)}, bf16[1,1,256,64]{2,3,1,0:T(8,128)(2,1)}, u32[]{:S(2)}) copy-start(bf16[1,1,256,64]{2,3,1,0:T(8,128)(2,1)} %param.31) | copy-start | bytes 98308
  11.5 70.8 %all-to-all-start = ((bf16[8,1,128,1024]{3,2,1,0:T(8,128)(2,1)}), bf16[8,1,128,1024]{3,2,1,0:T(8,128)(2,1)S(1)}, u32[]{:S(2)}, u32[]{:S(2)}) async-start(bf16[8,1,128,1024]{3,2,1,0:T(8,128)(2,1)} %broadcast_in_dim.210), calls=%async_computation | async-start | bytes 4194304 | tf_op jit(solution)/shard_map/all_to_all | solution.py:16
  20.2 69.5 %all-gather.9.cloned.1.call-start = ((), (), s32[]{:S(2)}) async-start(), calls=%async_computation.15 | async-start | bytes 1114112 | tf_op jit(solution)/shard_map/all_gather | solution.py:176
  44.2 41.5 %copy-start.59 = (f32[1,1,1,256]{3,2,1,0:T(1,128)}, f32[1,1,1,256]{3,2,1,0:T(1,128)S(1)}, u32[]{:S(2)}) copy-start(f32[1,1,1,256]{3,2,1,0:T(1,128)S(1)} %get-tuple-element.756) | copy-start | bytes 3076
  44.2 41.5 %copy-start.61 = (f32[1,1,1,256]{3,2,1,0:T(1,128)}, f32[1,1,1,256]{3,2,1,0:T(1,128)S(1)}, u32[]{:S(2)}) copy-start(f32[1,1,1,256]{3,2,1,0:T(1,128)S(1)} %get-tuple-element.757) | copy-start | bytes 3076
  44.2 41.5 %copy-start.63 = (f32[1,1,1,256]{3,2,1,0:T(1,128)}, f32[1,1,1,256]{3,2,1,0:T(1,128)S(1)}, u32[]{:S(2)}) copy-start(f32[1,1,1,256]{3,2,1,0:T(1,128)S(1)} %get-tuple-element.758) | copy-start | bytes 3076
  44.2 41.5 %copy-start.65 = (f32[1,1,1,256]{3,2,1,0:T(1,128)}, f32[1,1,1,256]{3,2,1,0:T(1,128)S(1)}, u32[]{:S(2)}) copy-start(f32[1,1,1,256]{3,2,1,0:T(1,128)S(1)} %get-tuple-element.759) | copy-start | bytes 3076
  44.2 49.4 %copy-start.51 = (f32[1,1,1,256]{3,2,1,0:T(1,128)}, f32[1,1,1,256]{3,2,1,0:T(1,128)S(1)}, u32[]{:S(2)}) copy-start(f32[1,1,1,256]{3,2,1,0:T(1,128)S(1)} %get-tuple-element.752) | copy-start | bytes 3076
  44.2 49.4 %copy-start.53 = (f32[1,1,1,256]{3,2,1,0:T(1,128)}, f32[1,1,1,256]{3,2,1,0:T(1,128)S(1)}, u32[]{:S(2)}) copy-start(f32[1,1,1,256]{3,2,1,0:T(1,128)S(1)} %get-tuple-element.753) | copy-start | bytes 3076
  44.2 49.4 %copy-start.55 = (f32[1,1,1,256]{3,2,1,0:T(1,128)}, f32[1,1,1,256]{3,2,1,0:T(1,128)S(1)}, u32[]{:S(2)}) copy-start(f32[1,1,1,256]{3,2,1,0:T(1,128)S(1)} %get-tuple-element.754) | copy-start | bytes 3076
  44.3 49.4 %copy-start.57 = (f32[1,1,1,256]{3,2,1,0:T(1,128)}, f32[1,1,1,256]{3,2,1,0:T(1,128)S(1)}, u32[]{:S(2)}) copy-start(f32[1,1,1,256]{3,2,1,0:T(1,128)S(1)} %get-tuple-element.755) | copy-start | bytes 3076
  62.0 23.6 %copy-start.24 = (bf16[1,1024,1,256]{3,1,2,0:T(8,128)(2,1)}, bf16[1,1024,1,256]{3,1,2,0:T(8,128)(2,1)S(1)}, u32[]{:S(2)}) copy-start(bf16[1,1024,1,256]{3,1,2,0:T(8,128)(2,1)S(1)} %all-gather.1) | copy-start | bytes 1572868
  82.4 7.3 copy-start
  87.6 4.5 copy-start.40
  87.7 4.5 copy-start.42
  87.7 4.5 copy-start.38
  95.4 215.4 %copy-start.71 = (f32[1,256]{1,0:T(1,128)S(1)}, f32[1,256]{1,0:T(1,128)}, u32[]{:S(2)}) copy-start(f32[1,256]{1,0:T(1,128)} %param.30) | copy-start | bytes 3076
  370.2 2.8 copy-start.33
  373.1 146.3 %copy-start.4 = (f32[1,128,1024]{2,1,0:T(8,128)}, f32[1,128,1024]{2,1,0:T(8,128)S(1)}, u32[]{:S(2)}) copy-start(f32[1,128,1024]{2,1,0:T(8,128)S(1)} %get-tuple-element.704) | copy-start | bytes 1572868
  373.1 146.3 %copy-start.67 = (f32[128]{0:T(128)}, f32[128]{0:T(128)S(1)}, u32[]{:S(2)}) copy-start(f32[128]{0:T(128)S(1)} %fusion.231) | copy-start | bytes 1540
  374.8 32.9 %copy-start.21 = (bf16[1,128,1024]{2,1,0:T(8,128)(2,1)S(1)}, bf16[1,128,1024]{2,1,0:T(8,128)(2,1)}, u32[]{:S(2)}) copy-start(bf16[1,128,1024]{2,1,0:T(8,128)(2,1)} %param.35) | copy-start | bytes 786436
  374.8 32.9 %all-to-all-start.2 = ((bf16[8,1,128,1024]{3,2,1,0:T(8,128)(2,1)}), bf16[8,1,128,1024]{3,2,1,0:T(8,128)(2,1)}, u32[]{:S(2)}, u32[]{:S(2)}) async-start(bf16[8,1,128,1024]{3,2,1,0:T(8,128)(2,1)} %broadcast_in_dim.211), calls=%async_computation.2 | async-start | bytes 4194304 | tf_op jit(solution)/shard_map/all_to_all | solution.py:16
  379.3 59.3 %all-gather.11.cloned.1.call-start = ((), (), s32[]{:S(2)}) async-start(), calls=%async_computation.16 | async-start | bytes 1671168 | tf_op jit(solution)/shard_map/all_gather | solution.py:179
  409.3 4.5 copy-start.36
  409.3 39.5 %all-to-all-start.4 = ((bf16[8,1,128,1024]{3,2,1,0:T(8,128)(2,1)}), bf16[8,1,128,1024]{3,2,1,0:T(8,128)(2,1)}, u32[]{:S(2)}, u32[]{:S(2)}) async-start(bf16[8,1,128,1024]{3,2,1,0:T(8,128)(2,1)} %broadcast_in_dim.212), calls=%async_computation.4 | async-start | bytes 4194304 | tf_op jit(solution)/shard_map/all_to_all | solution.py:16
  458.5 57.5 %all-to-all-start.5 = ((f32[8,1,128,1024]{3,2,1,0:T(8,128)}), f32[8,1,128,1024]{3,2,1,0:T(8,128)}, u32[]{:S(2)}, u32[]{:S(2)}) async-start(f32[8,1,128,1024]{3,2,1,0:T(8,128)} %convolution_bitcast_fusion.9), calls=%async_computation.5 | async-start | bytes 8388608 | tf_op jit(solution)/shard_map/all_to_all | solution.py:37
  465.3 561.4 %reduce-scatter.20.cloned.1.call-start = ((), (), s32[]{:S(2)}) async-start(), calls=%async_computation.19 | async-start | bytes 835584
  518.6 3.5 copy-start.8
  519.4 2.8 copy-start.75
  522.1 30.5 %all-to-all-start.6 = ((bf16[8,1,128,1024]{3,2,1,0:T(8,128)(2,1)}), bf16[8,1,128,1024]{3,2,1,0:T(8,128)(2,1)}, u32[]{:S(2)}, u32[]{:S(2)}) async-start(bf16[8,1,128,1024]{3,2,1,0:T(8,128)(2,1)} %broadcast_in_dim.214), calls=%async_computation.6 | async-start | bytes 4194304 | tf_op jit(solution)/shard_map/all_to_all | solution.py:16
  526.5 502.0 %all-reduce.30.cloned.1.call-start = ((), (), s32[]{:S(2)}) async-start(), calls=%async_computation.20 | async-start | bytes 3145728
  546.7 11.4 copy-start.27
  546.7 11.4 copy-start.72
  552.6 459.9 %all-to-all-start.3 = ((f32[8,1,128,1024]{3,2,1,0:T(8,128)}), f32[8,1,128,1024]{3,2,1,0:T(8,128)}, u32[]{:S(2)}, u32[]{:S(2)}) async-start(f32[8,1,128,1024]{3,2,1,0:T(8,128)} %convolution_bitcast_fusion.10), calls=%async_computation.3 | async-start | bytes 8388608 | tf_op jit(solution)/shard_map/all_to_all | solution.py:37
  557.8 507.6 %reduce-scatter.16.cloned.1.call-start = ((), (), s32[]{:S(2)}) async-start(), calls=%async_computation.17 | async-start | bytes 278528
  558.1 4.8 copy-start.11
  565.6 422.1 %copy-start.46 = (f32[16,1,1,64]{3,2,1,0:T(1,128)S(1)}, f32[16,1,1,64]{3,2,1,0:T(1,128)}, u32[]{:S(2)}) copy-start(f32[16,1,1,64]{3,2,1,0:T(1,128)} %get-tuple-element.712) | copy-start | bytes 12292
  565.6 423.5 %copy-start.48 = (f32[1,1024,1,1]{1,3,2,0:T(1,128)S(1)}, f32[1,1024,1,1]{1,3,2,0:T(1,128)}, u32[]{:S(2)}) copy-start(f32[1,1024,1,1]{1,3,2,0:T(1,128)} %get-tuple-element.708) | copy-start | bytes 12292
  565.6 423.5 %copy-start.35 = (f32[1,1024,1,2]{1,3,2,0:T(2,128)S(1)}, f32[1,1024,1,2]{1,3,2,0:T(2,128)}, u32[]{:S(2)}) copy-start(f32[1,1024,1,2]{1,3,2,0:T(2,128)} %copy-done.34) | copy-start | bytes 24580
  987.6 4.7 copy-start.16
  995.4 120.2 %reduce-scatter.18.cloned.1.call-start = ((), (), s32[]{:S(2)}) async-start(), calls=%async_computation.18 | async-start | bytes 557056
  996.1 3.4 copy-start.41
  996.1 3.4 copy-start.43
  996.1 3.4 copy-start.39
  1002.6 3.6 copy-start.23
  1012.5 6.8 copy-start.1
  1012.5 229.1 %all-to-all-start.7 = ((f32[8,1,128,1024]{3,2,1,0:T(8,128)}), f32[8,1,128,1024]{3,2,1,0:T(8,128)}, u32[]{:S(2)}, u32[]{:S(2)}) async-start(f32[8,1,128,1024]{3,2,1,0:T(8,128)} %bitcast.816), calls=%async_computation.7 | async-start | bytes 8388608 | tf_op jit(solution)/shard_map/all_to_all | solution.py:37
  1019.2 158.5 %reduce-scatter.12.cloned.1.call-start = ((), (), s32[]{:S(2)}) async-start(), calls=%async_computation.13 | async-start | bytes 557056 | tf_op jit(solution)/shard_map/reduce_scatter | solution.py:396
  1021.9 3.6 copy-start.81
  1021.9 218.0 %reduce-scatter.14.cloned.1.call-start = ((), (), s32[]{:S(2)}) async-start(), calls=%async_computation.14 | async-start | bytes 1114112 | tf_op jit(solution)/shard_map/reduce_scatter | solution.py:399
  1241.6 2.8 copy-start.37
  1241.6 2.8 copy-start.70
  1241.6 3.0 copy-start.47
  1241.6 3.0 copy-start.77
  1241.6 72.8 %copy-start.80 = (f32[128]{0:T(128)S(1)}, f32[128]{0:T(128)}, u32[]{:S(2)}) copy-start(f32[128]{0:T(128)} %copy-done.79) | copy-start | bytes 1540
  1241.6 72.8 %copy-start.5 = (f32[1,128,1024]{2,1,0:T(8,128)S(1)}, f32[1,128,1024]{2,1,0:T(8,128)}, u32[]{:S(2)}) copy-start(f32[1,128,1024]{2,1,0:T(8,128)} %copy-done.4) | copy-start | bytes 1572868
  1241.6 72.8 %copy-start.9 = (f32[128,1024]{1,0:T(8,128)S(1)}, f32[128,1024]{1,0:T(8,128)}, u32[]{:S(2)}) copy-start(f32[128,1024]{1,0:T(8,128)} %copy-done.8) | copy-start | bytes 1572868
  1241.6 72.8 %copy-start.22 = (bf16[1,128,1024]{2,1,0:T(8,128)(2,1)S(1)}, bf16[1,128,1024]{2,1,0:T(8,128)(2,1)}, u32[]{:S(2)}) copy-start(bf16[1,128,1024]{2,1,0:T(8,128)(2,1)} %param.35) | copy-start | bytes 786436
  1241.6 72.8 %copy-start.68 = (f32[128]{0:T(128)S(1)}, f32[128]{0:T(128)}, u32[]{:S(2)}) copy-start(f32[128]{0:T(128)} %copy-done.67) | copy-start | bytes 1540
  1241.6 72.8 %copy-start.76 = (f32[128]{0:T(128)S(1)}, f32[128]{0:T(128)}, u32[]{:S(2)}) copy-start(f32[128]{0:T(128)} %copy-done.75) | copy-start | bytes 1540
  (33 other events, 49.7 us)
Sparse Core Ops, SparseCore 0:
  22.7 36.0 all-gather.8
  381.9 35.3 all-gather.10
  477.0 59.0 reduce-scatter.19
  541.2 123.4 all-reduce.29
  995.5 58.2 reduce-scatter.15
  1056.1 59.4 reduce-scatter.17
  1118.6 59.0 reduce-scatter.11
  1180.2 59.7 reduce-scatter.13
where the time goes:
time: 1340 us; the launch traced here: 1320 us
  other arithmetic  370 us (28%)
  waiting for transfers between devices  244 us (18%)
  matrix products  244 us (18%)
  blocking collectives  242 us (18%)
  local copies, waits for them, and re-layouts  126 us (9%)
  starting transfers between devices  41.5 us (3%)
  loops' own time  36.8 us (3%)
  between operations  18.5 us (1%)
    another operation x112, other arithmetic, span_step(): jax.scipy.linalg.solve_triangular(system, right_side, lower=True, unit_di...  238 us
    psum x1, blocking collectives, packed_total(): so_far = lax.psum(vector, axis)  68.6 us
    reduce_scatter x1, waiting for transfers between devices, body(): lax.psum_scatter(stacked[1].astype(jnp.bfloat16), 'dp', scatter_dimension...  60.8 us
    reduce_scatter x1, waiting for transfers between devices, body(): lax.psum_scatter(stacked[0].astype(jnp.bfloat16), 'dp', scatter_dimension...  60.4 us
    all_to_all x1, blocking collectives, summed_on_arrival(): tiles = lax.all_to_all(split_up(x, dim, size), axis, 0, 0, tiled=True)  57 us
    unnamed x12, waiting for transfers between devices  50.3 us
    all_to_all x3, waiting for transfers between devices, summed_on_arrival(): tiles = lax.all_to_all(split_up(x, dim, size), axis, 0, 0, tiled=True)  39.1 us
    squeeze x64, local copies, waits for them, and re-layouts, delta_head(): final_memory, outputs = lax.scan(jax.checkpoint(span_step), start, blocks)  37.6 us
  transfers between devices with their start and end apart: 15, of which 6 were waited for; matrix products, arithmetic and copies ran while one was open for 38% of the time, Pallas kernels for 0%

commit v1 on v0

v1 whole, which is shorter than its diff:
```python
import functools

import jax
import jax.numpy as jnp
from jax import lax
from jax.experimental import pallas as pl
from jax.experimental.pallas import tpu as pltpu
from jax.sharding import PartitionSpec as P
C = 128
HI = lax.Precision.HIGHEST
LO = lax.Precision.DEFAULT
F32 = jnp.float32
NN = (((1,), (0,)), ((), ()))
NT = (((1,), (1,)), ((), ()))
TN = (((0,), (0,)), ((), ()))


def mm(a, b, dims=NN, precision=HI):
    return lax.dot_general(a, b, dims, precision=precision, preferred_element_type=F32)


def chunk_masks():
    row = lax.broadcasted_iota(jnp.int32, (C, C), 0)
    col = lax.broadcasted_iota(jnp.int32, (C, C), 1)
    return row, col


def decay_parts(g, row, col):
    lower = (row >= col).astype(F32)
    cum = mm(lower, g)
    table = jnp.where(row >= col, jnp.exp(jnp.where(row >= col, cum - cum.T, 0.0)), 0.0)
    last = cum[C - 1 : C, :]
    return table, jnp.exp(cum), jnp.exp(last - cum), jnp.exp(last)


def wide(x):
    return jnp.concatenate([x, x], axis=1)


def inverse_many(systems, row, col, prec):
    eye = (row == col).astype(F32)
    near = (row // 8) == (col // 8)
    a1 = [jnp.where(near, a, 0.0) for a in systems]
    a2 = [mm(a, a, precision=prec) for a in a1]
    x = [eye - a for a in a1]
    a4 = [mm(a, a, precision=prec) for a in a2]
    x = [y + mm(y, a, precision=prec) for y, a in zip(x, a2)]
    x = [y + mm(y, a, precision=prec) for y, a in zip(x, a4)]
    size = 8
    while size < C:
        pick = ((row // (2 * size)) == (col // (2 * size))) & ((row // size) != (col // size))
        off = [jnp.where(pick, a, 0.0) for a in systems]
        y = [mm(o, t, precision=prec) for o, t in zip(off, x)]
        x = [t - mm(t, z, precision=prec) for t, z in zip(x, y)]
        size *= 2
    return x


def fwd_kernel(P_, group, q_ref, k_ref, v_ref, b_ref, g_ref, o_ref, t_ref, u_ref, s_ref, f_ref, w_ref, z_ref):
    nb = q_ref.shape[0] // C
    row, col = chunk_masks()

    def first(i, _):
        cs = [pl.ds(pl.multiple_of((i * group + j) * C, C), C) for j in range(group)]
        q = [q_ref[c, :] for c in cs]
        k = [k_ref[c, :] for c in cs]
        v = [v_ref[c, :] for c in cs]
        b = [b_ref[c, :] for c in cs]
        parts = [decay_parts(g_ref[c, :], row, col) for c in cs]
        kk = [mm(x, x, NT, P_["kk"]) for x in k]
        system = [jnp.where(row > col, bb * x * p[0], 0.0) for bb, x, p in zip(b, kk, parts)]
        t = inverse_many(system, row, col, P_["inv"])
        w = [mm(tt, bb * p[1] * x, precision=P_["w"]) for tt, bb, p, x in zip(t, b, parts, k)]
        u0 = [mm(tt, wide(bb) * x, precision=P_["u"]) for tt, bb, x in zip(t, b, v)]
        kd = [x * p[2] for x, p in zip(k, parts)]
        eye = (row == col).astype(F32)
        for c, kdd, ww, uu, tt, p in zip(cs, kd, w, u0, t, parts):
            t_ref[c, :] = tt
            w_ref[c, :] = ww
            u_ref[c, :] = uu
            f_ref[c, :] = eye * p[3] - mm(kdd, ww, TN, P_["f"])
            z_ref[c, :] = mm(kdd, uu, TN, P_["z"])
        return 0

    lax.fori_loop(0, nb // group, first, 0)
    state = jnp.zeros((C, v_ref.shape[1]), F32)
    for i in range(nb):
        c = pl.ds(i * C, C)
        s_ref[c, :] = state
        if i < nb - 1:
            state = z_ref[c, :] + mm(f_ref[c, :], state, precision=P_["chain"])

    def last(i, _):
        cs = [pl.ds(pl.multiple_of((i * group + j) * C, C), C) for j in range(group)]
        for c in cs:
            q, k, s = q_ref[c, :], k_ref[c, :], s_ref[c, :]
            table, scale, _, _ = decay_parts(g_ref[c, :], row, col)
            u = u_ref[c, :] - mm(w_ref[c, :], s, precision=P_["ws"])
            u_ref[c, :] = u
            scores = mm(q, k, NT, P_["qk"]) * table
            o_ref[c, :] = mm(q * scale, s, precision=P_["o"]) + mm(scores, u, precision=P_["o"])
        return 0

    lax.fori_loop(0, nb // group, last, 0)


def bwd_kernel(P_, group, q_ref, k_ref, v_ref, b_ref, g_ref, t_ref, u_ref, s_ref, f_ref, w_ref, do_ref,
               dq_ref, dk_ref, dv_ref, db_ref, dg_ref, ds_ref, x_ref):
    nb = q_ref.shape[0] // C
    row, col = chunk_masks()

    def first(i, _):
        cs = [pl.ds(pl.multiple_of((i * group + j) * C, C), C) for j in range(group)]
        for c in cs:
            q, k, do = q_ref[c, :], k_ref[c, :], do_ref[c, :]
            table, scale, _, _ = decay_parts(g_ref[c, :], row, col)
            scores = mm(q, k, NT, P_["qk"]) * table
            x = mm(scores, do, TN, P_["bx"])
            x_ref[c, :] = x
            ds_ref[c, :] = mm(q * scale, do, TN, P_["bx"]) - mm(w_ref[c, :], x, TN, P_["bx"])
        return 0

    lax.fori_loop(0, nb // group, first, 0)
    carry = jnp.zeros((C, v_ref.shape[1]), F32)
    for i in reversed(range(nb)):
        c = pl.ds(i * C, C)
        own = ds_ref[c, :]
        ds_ref[c, :] = carry
        if i > 0:
            carry = own + mm(f_ref[c, :], carry, TN, P_["chain"])

    def last(i, _):
        cs = [pl.ds(pl.multiple_of((i * group + j) * C, C), C) for j in range(group)]
        for c in cs:
            q, k, v, b, do = q_ref[c, :], k_ref[c, :], v_ref[c, :], b_ref[c, :], do_ref[c, :]
            t, u, s, ds = t_ref[c, :], u_ref[c, :], s_ref[c, :], ds_ref[c, :]
            table, scale, tail, total = decay_parts(g_ref[c, :], row, col)
            p = P_["bl"]
            qk = mm(q, k, NT, p)
            kk = mm(k, k, NT, p)
            ks = mm(k, s, precision=p)
            qs = mm(q, s, precision=p)
            kd = k * tail
            du = x_ref[c, :] + mm(kd, ds, precision=p)
            dr = mm(t, du, TN, P_["bt"])
            dp = jnp.where(row >= col, mm(do, u, NT, p), 0.0)
            da = jnp.where(row > col, -mm(dr, u, NT, p), 0.0)
            dqk = dp * table
            dkk = da * b * table
            n = dqk * qk + dkk * kk
            dkd = mm(u, ds, NT, p)
            dq_ref[c, :] = scale * mm(do, s, NT, p) + mm(dqk, k, precision=p)
            bdr = wide(b) * dr
            dk_ref[c, :] = (
                mm(dqk, q, TN, p)
                + mm(dkk, k, precision=p)
                + mm(dkk, k, TN, p)
                + dkd * tail
                - scale * mm(bdr, s, NT, p)
            )
            dv_ref[c, :] = bdr
            sc2 = wide(scale)
            db = jnp.sum(dr * (v - sc2 * ks), 1, keepdims=True) + jnp.sum(da * table * kk, 1, keepdims=True)
            db_ref[c, :] = jnp.broadcast_to(db, (C, C))
            tails = jnp.sum(dkd * kd, 1, keepdims=True)
            dcum = (
                jnp.sum(n, 1, keepdims=True)
                - jnp.sum(n.T, 1, keepdims=True)
                + jnp.sum(sc2 * (do * qs - bdr * ks), 1, keepdims=True)
                - tails
            )
            dcum = jnp.broadcast_to(dcum, (C, C))
            extra = jnp.sum(tails) + jnp.sum(ds * s * wide(jnp.broadcast_to(total, (C, C))))
            upper = (row <= col).astype(F32)
            dg_ref[c, :] = mm(upper, dcum) + extra
        return 0

    lax.fori_loop(0, nb // group, last, 0)


KEYS = ("kk", "inv", "w", "u", "f", "z", "chain", "ws", "qk", "o", "bx", "bl", "bt")
PRECS = {key: HI for key in KEYS}
BF = jnp.bfloat16
EPS = 1e-06
GATED_EPS = 1e-05
DP, TP = "dp", "tensor"


def in_vmem(n):
    return [pl.BlockSpec(memory_space=pltpu.VMEM)] * n


def delta_fwd(q, k, v, b, g):
    n, dv = v.shape
    sh = lambda w: jax.ShapeDtypeStruct((n, w), F32)
    return pl.pallas_call(
        functools.partial(fwd_kernel, PRECS, 4),
        out_shape=[sh(dv), sh(C), sh(dv), sh(dv), sh(C), sh(C)],
        in_specs=in_vmem(5),
        out_specs=in_vmem(6),
        scratch_shapes=[pltpu.VMEM((n, dv), F32)],
        compiler_params=pltpu.CompilerParams(vmem_limit_bytes=48 * 2**20),
        name="delta_forward",
    )(q, k, v, b, g)


def delta_bwd(q, k, v, b, g, t, u, s, f, w, do):
    n, dv = v.shape
    sh = lambda w: jax.ShapeDtypeStruct((n, w), F32)
    return pl.pallas_call(
        functools.partial(bwd_kernel, PRECS, 2),
        out_shape=[sh(C), sh(C), sh(dv), sh(C), sh(C)],
        in_specs=in_vmem(11),
        out_specs=in_vmem(5),
        scratch_shapes=[pltpu.VMEM((n, dv), F32), pltpu.VMEM((n, dv), F32)],
        compiler_params=pltpu.CompilerParams(vmem_limit_bytes=48 * 2**20),
        name="delta_backward",
    )(q, k, v, b, g, t, u, s, f, w, do)


def spread_columns(x):
    return jnp.broadcast_to(x[:, None], (x.shape[0], C))


@jax.custom_vjp
def delta_rule(q, k, v, b, g):
    return delta_rule_fwd(q, k, v, b, g)[0]


def delta_rule_fwd(q, k, v, b, g):
    b, g = spread_columns(b), spread_columns(g)
    o, t, u, s, f, w = delta_fwd(q, k, v, b, g)
    return o, (q, k, v, b, g, t, u, s, f, w)


def delta_rule_bwd(kept, do):
    dq, dk, dv, db, dg = delta_bwd(*kept, do)
    return dq, dk, dv, db[:, 0], dg[:, 0]


delta_rule.defvjp(delta_rule_fwd, delta_rule_bwd)


def norm_rows(values, gain, offset=EPS):
    return values * lax.rsqrt(jnp.mean(values * values, -1, keepdims=True) + offset) * gain


def causal_conv(inputs, taps):
    length = inputs.shape[0]
    padded = jnp.pad(inputs, ((taps.shape[0] - 1, 0), (0, 0)))
    summed = padded[0:length] * taps[0]
    for shift_at in range(1, taps.shape[0]):
        summed = summed + padded[shift_at : shift_at + length] * taps[shift_at]
    return summed


def mixer_core(qk_pre, vg_pre, bd_pre, conv_qk, conv_v, decay_log, decay_bias, out_gain):
    dk, dv = qk_pre.shape[-1] // 2, vg_pre.shape[-1] // 2
    rows = jax.nn.silu(causal_conv(qk_pre, conv_qk))
    q, k = rows[:, :dk], rows[:, dk:]
    q = q * lax.rsqrt(jnp.sum(q * q, -1, keepdims=True) + EPS) * dk ** (-0.5)
    k = k * lax.rsqrt(jnp.sum(k * k, -1, keepdims=True) + EPS)
    v = jax.nn.silu(causal_conv(vg_pre[:, :dv], conv_v))
    b = jax.nn.sigmoid(bd_pre[:, 0])
    g = -jnp.exp(decay_log) * jax.nn.softplus(bd_pre[:, 1] + decay_bias)
    return norm_rows(delta_rule(q, k, v, b, g), out_gain, GATED_EPS) * jax.nn.silu(vg_pre[:, dv:])


def dot(a, b, dims=NN):
    return lax.dot_general(a, b, dims, preferred_element_type=F32)


def gather(x, axis):
    copies = jnp.broadcast_to(x, (lax.axis_size(axis), *x.shape))
    tiles = lax.all_to_all(copies, axis, split_axis=0, concat_axis=0, tiled=True)
    return tiles.reshape(-1, x.shape[1])


def scatter_sum(x, axis):
    n = lax.axis_size(axis)
    tiles = x.astype(BF).reshape(n, x.shape[0] // n, x.shape[1])
    tiles = lax.all_to_all(tiles, axis, 0, 0, tiled=True)
    return jnp.sum(tiles.astype(F32), axis=0)


def body(
    block_input,
    mixer_gain,
    query_key_weight,
    value_gate_weight,
    beta_decay_weight,
    conv_query_key,
    conv_value,
    decay_log,
    decay_bias,
    out_gain,
    out_weight,
    forward_gain,
    gate_up_weight,
    down_weight,
    out_cotangent,
):
    stream = block_input[0].astype(F32)
    nqk, nvg, nbd = query_key_weight.shape[-1], value_gate_weight.shape[-1], beta_decay_weight.shape[-1]
    ff = gate_up_weight.shape[-1]
    nout = out_weight.shape[2]
    first_pack = jnp.concatenate(
        [query_key_weight[0, :, 0], value_gate_weight[0, :, 0], beta_decay_weight[0, :, 0]], 1
    )
    second_pack = jnp.concatenate(
        [out_weight[0, 0].T, gate_up_weight[0].reshape(-1, 2 * ff), down_weight[0].T], 1
    )
    w_in = gather(first_pack, DP)
    rows = gather(norm_rows(stream, mixer_gain[0]).astype(BF), TP)
    g_rows = gather(out_cotangent[0], TP)
    w_rest = gather(second_pack, DP)
    w_out, w_gu, w_down = w_rest[:, :nout], w_rest[:, nout : nout + 2 * ff], w_rest[:, nout + 2 * ff :]
    w_qk, w_vg, w_bd = w_in[:, :nqk], w_in[:, nqk : nqk + nvg], w_in[:, nqk + nvg :]

    mixed, core_back = jax.vjp(
        mixer_core,
        dot(rows, w_qk),
        dot(rows, w_vg),
        dot(rows, w_bd),
        conv_query_key[0, :, 0],
        conv_value[0, :, 0],
        decay_log[0, 0],
        decay_bias[0, 0],
        out_gain[0],
    )
    mixed = mixed.astype(BF)
    before_forward = stream + scatter_sum(dot(mixed, w_out, NT), TP)
    forward_rows = gather(norm_rows(before_forward, forward_gain[0]).astype(BF), TP)
    gate = dot(forward_rows, w_gu[:, :ff])
    up = dot(forward_rows, w_gu[:, ff:])
    s = jax.nn.sigmoid(gate)
    hidden = (gate * s * up).astype(BF)
    grad_hidden = dot(g_rows, w_down)
    grad_gu = jnp.concatenate(
        [(grad_hidden * up * s * (1.0 + gate * (1.0 - s))).astype(BF), (grad_hidden * gate * s).astype(BF)], 1
    )
    grad_normed = scatter_sum(dot(grad_gu, w_gu, NT), TP)
    _, norm_back = jax.vjp(norm_rows, before_forward, forward_gain[0])
    grad_before, grad_fgain = norm_back(grad_normed)
    grad_stream = out_cotangent[0].astype(F32) + grad_before
    m_rows = gather(grad_stream.astype(BF), TP)
    output = before_forward + scatter_sum(dot(hidden, w_down, NT), TP)
    grad_rest = jnp.concatenate(
        [dot(m_rows, mixed, TN), dot(forward_rows, grad_gu, TN), dot(g_rows, hidden, TN)], 1
    )
    own_rest = scatter_sum(grad_rest, DP)

    d_qk, d_vg, d_bd, grad_cqk, grad_cv, grad_dlog, grad_dbias, grad_ogain = core_back(dot(m_rows, w_out))
    d_in = jnp.concatenate([d_qk.astype(BF), d_vg.astype(BF), d_bd.astype(BF)], 1)
    grad_normed = scatter_sum(dot(d_in, w_in, NT), TP)
    own_in = scatter_sum(dot(rows, d_in, TN), DP)
    _, norm_back = jax.vjp(norm_rows, stream, mixer_gain[0])
    grad_before, grad_mgain = norm_back(grad_normed)
    input_grad = grad_stream + grad_before

    heads = lax.psum((grad_cqk, grad_cv, grad_dlog, grad_dbias), DP)
    gains = lax.psum(jnp.concatenate([grad_mgain, grad_fgain, grad_ogain]), (DP, TP))
    d = grad_mgain.shape[0]
    return (
        output[None],
        input_grad[None],
        gains[None, :d],
        own_in[None, :, None, :nqk],
        own_in[None, :, None, nqk : nqk + nvg],
        own_in[None, :, None, nqk + nvg :],
        heads[0][None, :, None],
        heads[1][None, :, None],
        heads[2][None, None],
        heads[3][None, None],
        gains[None, 2 * d :],
        own_rest[:, :nout].T[None, None],
        gains[None, d : 2 * d],
        own_rest[:, nout : nout + 2 * ff].reshape(1, -1, 2, ff),
        own_rest[:, nout + 2 * ff :].T[None],
    )


def solution(mesh):
    placed = (
        P("dp", "tensor", None),
        P(),
        P(None, "dp", "tensor", None),
        P(None, "dp", "tensor", None),
        P(None, "dp", "tensor", None),
        P(None, None, "tensor", None),
        P(None, None, "tensor", None),
        P(None, "tensor"),
        P(None, "tensor"),
        P(),
        P(None, "tensor", None, "dp"),
        P(),
        P(None, "dp", None, "tensor"),
        P(None, "tensor", "dp"),
        P("dp", "tensor", None),
    )
    return jax.shard_map(
        body,
        mesh=mesh,
        in_specs=placed,
        out_specs=(
            P("dp", "tensor", None),
            P("dp", "tensor", None),
            P(),
            P(None, "dp", "tensor", None),
            P(None, "dp", "tensor", None),
            P(None, "dp", "tensor", None),
            P(None, None, "tensor", None),
            P(None, None, "tensor", None),
            P(None, "tensor"),
            P(None, "tensor"),
            P(),
            P(None, "tensor", None, "dp"),
            P(),
            P(None, "dp", None, "tensor"),
            P(None, "tensor", "dp"),
        ),
        check_vma=False,
    )
```

time: 1340 us -> 583 us (0.44)
  other arithmetic: 370 us -> 31.6 us
  matrix products: 244 us -> 49.1 us
  waiting for transfers between devices: 244 us -> 132 us
  blocking collectives: 242 us -> 183 us
  local copies, waits for them, and re-layouts: 126 us -> 67.1 us
  Pallas kernels: 0 us -> 47.1 us
  loops' own time: 36.8 us -> 0 us
  starting transfers between devices: 41.5 us -> 58.6 us
  between operations: 18.5 us -> 3.81 us
    another operation x195 -> x1, other arithmetic: 276 us -> 0.35 us  [the longest x112 238 us: span_step(): jax.scipy.linalg.solve_triangular(system, right_side, lower=True, unit_di...]
    dot_general x386 -> x15, matrix products: 217 us -> 49.1 us  [dot(): return lax.dot_general(a, b, dims, preferred_element_type=F32)]
    reduce_scatter x2 -> x0, waiting for transfers between devices: 121 us -> none  [the longest x1 60.8 us: body(): lax.psum_scatter(stacked[1].astype(jnp.bfloat16), 'dp', scatter_dimension...]
    all_gather x4 -> x0, blocking collectives: 84.3 us -> none  [the longest x1 24.8 us: body(): lax.all_gather(down_weight[layer_num], 'dp', axis=1, tiled=True)]
    all_to_all x7 -> x10, waiting for transfers between devices: 72.7 us -> 132 us  [the longest x6 113 us: gather(): lax.all_to_all(copies, axis, split_axis=0, concat_axis=0, tiled=True)]
    unnamed x12 -> x0, waiting for transfers between devices: 50.3 us -> none
    pallas_call x0 -> x2, Pallas kernels: none -> 47.1 us  [the longest x1 27.3 us: mixer_core(): delta_rule(q, k, v, b, g)]
    reduce_sum x87 -> x9, other arithmetic: 51.1 us -> 10.9 us  [the longest x6 9.55 us: scatter_sum(): return jnp.sum(tiles.astype(F32), axis=0)]
  transfers between devices with their start and end apart: 15 -> 10, of which waited for: 6 -> 7; matrix products, arithmetic and copies ran while one was open for 38% -> 17% of each run, Pallas kernels for 0% -> 8%
where the time goes in v1:
time: 583 us; the launch traced here: 572 us
  blocking collectives  183 us (31%)
  waiting for transfers between devices  132 us (23%)
  local copies, waits for them, and re-layouts  67.1 us (12%)
  starting transfers between devices  58.6 us (10%)
  matrix products  49.1 us (8%)
  Pallas kernels  47.1 us (8%)
  other arithmetic  31.6 us (5%)
    all_to_all x6, waiting for transfers between devices, gather(): lax.all_to_all(copies, axis, split_axis=0, concat_axis=0, tiled=True)  113 us
    psum x1, blocking collectives, body(): lax.psum(jnp.concatenate([grad_mgain, grad_fgain, grad_ogain]), (DP, TP))  65.1 us
    all_to_all x2, blocking collectives, scatter_sum(): tiles = lax.all_to_all(tiles, axis, 0, 0, tiled=True)  63.4 us
    psum x1, blocking collectives, body(): heads = lax.psum((grad_cqk, grad_cv, grad_dlog, grad_dbias), DP)  54.3 us
    dot_general x15, matrix products, dot(): return lax.dot_general(a, b, dims, preferred_element_type=F32)  49.1 us
    all_to_all x6, starting transfers between devices, gather(): lax.all_to_all(copies, axis, split_axis=0, concat_axis=0, tiled=True)  34.2 us
    pallas_call x1, Pallas kernels, mixer_core(): delta_rule(q, k, v, b, g)  27.3 us
    all_to_all x4, starting transfers between devices, scatter_sum(): tiles = lax.all_to_all(tiles, axis, 0, 0, tiled=True)  24.4 us
  transfers between devices with their start and end apart: 10, of which 7 were waited for; matrix products, arithmetic and copies ran while one was open for 17% of the time, Pallas kernels for 8%

profile of v1, /device:TPU:1, one launch (start us, length us, event | category | flops | bytes accessed | tf_op | source)
XLA Modules:
  0.0 572.1 jit_solution(3838669800914192175)
XLA Ops:
  2.3 1.5 broadcast_in_dim.107
  3.8 7.0 %all-to-all-start.1 = ((bf16[16,64,770]{2,1,0:T(8,128)(2,1)}), bf16[16,64,770]{2,1,0:T(8,128)(2,1)S(1)}, u32[]{:S(2)}, u32[]{:S(2)}) async-start(bf16[16,64,770]{2,1,0:T(8,128)(2,1)} %broadcast_in_dim.107), calls=%async_computation.1 | async-start | bytes 3670016 | tf_op jit(solution)/shard_map/all_to_all | solution.py:275
  11.5 23.6 %all-to-all-done.1 = bf16[16,64,770]{2,1,0:T(8,128)(2,1)S(1)} async-done(((bf16[16,64,770]{2,1,0:T(8,128)(2,1)}), bf16[16,64,770]{2,1,0:T(8,128)(2,1)S(1)}, u32[]{:S(2)}, u32[]{:S(2)}) %all-to-all-start.1) | async-done | bytes 1576992 | tf_op jit(solution)/shard_map/all_to_all | solution.py:275
  35.1 1.8 broadcast_in_dim.106
  36.9 7.5 %all-to-all-start = ((bf16[8,128,1024]{2,1,0:T(8,128)(2,1)}), bf16[8,128,1024]{2,1,0:T(8,128)(2,1)S(1)}, u32[]{:S(2)}, u32[]{:S(2)}) async-start(bf16[8,128,1024]{2,1,0:T(8,128)(2,1)} %broadcast_in_dim.106), calls=%async_computation | async-start | bytes 4194304 | tf_op jit(solution)/shard_map/all_to_all | solution.py:275
  46.1 24.5 %all-to-all-done = bf16[8,128,1024]{2,1,0:T(8,128)(2,1)S(1)} async-done(((bf16[8,128,1024]{2,1,0:T(8,128)(2,1)}), bf16[8,128,1024]{2,1,0:T(8,128)(2,1)S(1)}, u32[]{:S(2)}, u32[]{:S(2)}) %all-to-all-start) | async-done | bytes 2097184 | tf_op jit(solution)/shard_map/all_to_all | solution.py:275
  70.6 2.1 broadcast_in_dim.112
  72.7 5.4 all-to-all-start.2
  78.1 1.9 fusion.42
  80.0 1.3 fusion.10
  81.3 1.7 fusion.14
  83.5 1.9 copy-done.20
  87.9 2.0 fusion.13
  90.3 19.8 %jvp_delta_forward_.1 = (f32[1024,256]{1,0:T(8,128)S(1)}, f32[1024,128]{1,0:T(8,128)S(1)}, f32[1024,256]{1,0:T(8,128)S(1)}, f32[1024,256]{1,0:T(8,128)}, f32[102...) custom-call(f32[1024,128]{1,0:T(8,128)S(1)} %get-tuple-element.85.q_ref, f32[1024,128]{1,0:T(8,128)S(1)} %get-tuple-element.84.k_ref, ...), custom_call_target="tpu_custom_call" | custom-call | tf_op jit(solution)/shard_map/jvp(delta_forward)/pallas_call | solution.py:196
  114.8 1.4 all-to-all-done.2
  116.2 1.9 convolution_convert_fusion.2
  118.2 31.3 %all_to_all.60 = bf16[8,128,1024]{2,1,0:T(8,128)(2,1)} all-to-all(bf16[8,128,1024]{2,1,0:T(8,128)(2,1)S(1)} %bitcast.152), channel_id=1, replica_groups=mesh['dp'=16,'tensor'=8] {'tensor'}, dimensions={0} | all-to-all | bytes 4194304 | tf_op jit(solution)/shard_map/all_to_all | solution.py:282
  149.5 1.6 broadcast_in_dim.114
  151.0 4.4 all-to-all-start.6
  155.4 2.0 convert_reduce_fusion.4
  159.1 1.8 copy.78
  160.9 20.3 %all-to-all-done.6 = bf16[8,128,1024]{2,1,0:T(8,128)(2,1)} async-done(((bf16[8,128,1024]{2,1,0:T(8,128)(2,1)}), bf16[8,128,1024]{2,1,0:T(8,128)(2,1)}, u32[]{:S(2)}, u32[]{:S(2)}) %all-to-all-start.6) | async-done | bytes 2097184 | tf_op jit(solution)/shard_map/all_to_all | solution.py:275
  181.2 2.5 broadcast_in_dim.113
  183.7 5.6 all-to-all-start.4
  189.3 4.5 convolution_bitcast_fusion
  193.7 21.8 %all-to-all-done.4 = bf16[8,128,1024]{1,2,0:T(8,128)(2,1)} async-done(((bf16[8,128,1024]{1,2,0:T(8,128)(2,1)}), bf16[8,128,1024]{1,2,0:T(8,128)(2,1)}, u32[]{:S(2)}, u32[]{:S(2)}) %all-to-all-start.4) | async-done | bytes 2097184 | tf_op jit(solution)/shard_map/all_to_all | solution.py:275
  215.5 3.9 copy.79
  219.4 3.3 fusion.15
  222.8 3.6 multiply_convert_fusion.1
  226.4 3.8 convolution_convert_fusion.3
  230.2 32.0 %all_to_all.61 = bf16[8,128,1024]{2,1,0:T(8,128)(2,1)S(1)} all-to-all(bf16[8,128,1024]{2,1,0:T(8,128)(2,1)S(1)} %bitcast.164), channel_id=1, replica_groups=mesh['dp'=16,'tensor'=8] {'tensor'}, dimensions={0} | all-to-all | bytes 4194304 | tf_op jit(solution)/shard_map/all_to_all | solution.py:282
  265.0 1.8 copy.80
  266.8 2.5 broadcast_in_dim.117
  269.3 4.3 all-to-all-start.8
  273.7 4.2 convolution_convert_fusion
  277.9 21.6 %all-to-all-done.8 = bf16[8,128,1024]{1,2,0:T(8,128)(2,1)} async-done(((bf16[8,128,1024]{1,2,0:T(8,128)(2,1)}), bf16[8,128,1024]{1,2,0:T(8,128)(2,1)}, u32[]{:S(2)}, u32[]{:S(2)}) %all-to-all-start.8) | async-done | bytes 2097184 | tf_op jit(solution)/shard_map/all_to_all | solution.py:275
  299.5 5.5 all-to-all-start.5
  305.0 3.9 copy.81
  309.0 4.0 multiply_reduce_fusion.8
  313.0 1.4 add_add_fusion.do_ref
  314.4 27.3 %transpose_jvp_delta_backward__.1 = (f32[1024,128]{1,0:T(8,128)S(1)}, f32[1024,128]{1,0:T(8,128)S(1)}, f32[1024,256]{1,0:T(8,128)}, f32[1024,128]{1,0:T(8,128)S(1)}, f32[1024,128]{1,0:T(8,128)S(1)}) custom-call(f32[1024,128]{1,0:T(8,128)S(1)} %get-tuple-element.85.q_ref, f32[1024,128]{1,0:T(8,128)S(1)} %get-tuple-element.84.k_ref, ...), custom_call_target="tpu_custom_call" | custom-call | tf_op jit(solution)/shard_map/transpose(jvp(delta_backward))/pallas_call | solution.py:266
  352.2 3.1 convolution_convert_fusion.4
  355.3 3.8 copy.85
  359.0 5.7 %all-to-all-start.10 = ((bf16[16,64,770]{2,1,0:T(8,128)(2,1)}), bf16[16,64,770]{2,1,0:T(8,128)(2,1)S(1)}, u32[]{:S(2)}, u32[]{:S(2)}) async-start(bf16[16,64,770]{2,1,0:T(8,128)(2,1)} %bitcast.153), calls=%async_computation.10 | async-start | bytes 3670016 | tf_op jit(solution)/shard_map/all_to_all | solution.py:282
  364.8 5.4 convolution_convert_fusion.1
  370.2 19.0 %all-to-all-done.10 = bf16[16,64,770]{2,1,0:T(8,128)(2,1)S(1)} async-done(((bf16[16,64,770]{2,1,0:T(8,128)(2,1)}), bf16[16,64,770]{2,1,0:T(8,128)(2,1)S(1)}, u32[]{:S(2)}, u32[]{:S(2)}) %all-to-all-start.10) | async-done | bytes 1576992 | tf_op jit(solution)/shard_map/all_to_all | solution.py:282
  389.1 1.2 copy-done.25
  390.4 7.8 %all-to-all-start.9 = ((bf16[8,128,1024]{2,1,0:T(8,128)(2,1)}), bf16[8,128,1024]{2,1,0:T(8,128)(2,1)S(1)}, u32[]{:S(2)}, u32[]{:S(2)}) async-start(bf16[8,128,1024]{2,1,0:T(8,128)(2,1)} %bitcast.161), calls=%async_computation.9 | async-start | bytes 4194304 | tf_op jit(solution)/shard_map/all_to_all | solution.py:282
  398.2 3.4 fusion.2
  401.6 1.5 copy.89
  403.0 4.0 copy.88
  407.0 4.9 convolution_convert_fusion.5
  411.9 3.9 copy.87
  415.9 3.2 convolution_convert_fusion.7
  419.1 5.3 concatenate.28
  424.4 5.3 all-to-all-start.11
  429.7 2.8 convert_reduce_fusion.3
  433.9 54.3 %all-reduce.24 = (f32[1,4,1,256]{3,2,1,0:T(1,128)}, f32[1,4,1,256]{3,2,1,0:T(1,128)}, f32[1,1]{1,0:T(1,128)}, f32[1,1]{1,0:T(1,128)}) all-reduce(f32[1,4,1,256]{3,2,1,0:T(1,128)S(1)} %broadcast_in_dim.126, f32[1,4,1,256]{3,2,1,0:T(1,128)S(1)} %broadcast_in_dim.127, f32[1,1]{1,0:T(1,128)} %bitcast.48, ...), channel_id=1, replica_groups=mesh['dp'=16,'tensor'=8] {'dp'}, use_global_device_ids=true, to_apply=%region_23.24 | all-reduce | flops 2050 | bytes 16400 | tf_op jit(solution)/shard_map/psum | solution.py:361
  488.1 1.8 convert_reduce_fusion.5
  491.2 1.5 copy.86
  493.4 1.5 broadcast_in_dim.123
  497.6 65.1 %psum.35 = f32[2304]{0:T(1024)S(1)} all-reduce(f32[2304]{0:T(1024)S(1)} %pad_maximum_fusion.7), channel_id=1, replica_groups=mesh['dp'=16,'tensor'=8] {'dp','tensor'}, use_global_device_ids=true, to_apply=%region_17.18 | all-reduce | flops 2304 | bytes 18432 | tf_op jit(solution)/shard_map/psum | solution.py:362
  564.5 2.6 fusion.32
  567.1 2.3 convert_reduce_fusion
  (173 shorter events, 35.1 us)
Async XLA Ops:
  3.8 7.0 %copy-start.12 = (bf16[1,128,1024]{2,1,0:T(8,128)(2,1)S(1)}, bf16[1,128,1024]{2,1,0:T(8,128)(2,1)}, u32[]{:S(2)}) copy-start(bf16[1,128,1024]{2,1,0:T(8,128)(2,1)} %param.15) | copy-start | bytes 786436
  3.8 7.6 %copy-start.44 = (f32[1,1024]{1,0:T(1,128)S(1)}, f32[1,1024]{1,0:T(1,128)}, u32[]{:S(2)}) copy-start(f32[1,1024]{1,0:T(1,128)} %param.16) | copy-start | bytes 12292
  3.8 31.3 %all-to-all-start.1 = ((bf16[16,64,770]{2,1,0:T(8,128)(2,1)}), bf16[16,64,770]{2,1,0:T(8,128)(2,1)S(1)}, u32[]{:S(2)}, u32[]{:S(2)}) async-start(bf16[16,64,770]{2,1,0:T(8,128)(2,1)} %broadcast_in_dim.107), calls=%async_computation.1 | async-start | bytes 3670016 | tf_op jit(solution)/shard_map/all_to_all | solution.py:275
  11.4 23.7 %copy-start.46 = (f32[128]{0:T(128)}, f32[128]{0:T(128)S(1)}, u32[]{:S(2)}) copy-start(f32[128]{0:T(128)S(1)} %fusion.60) | copy-start | bytes 1540
  35.1 1.8 copy-start.31
  36.9 8.9 %copy-start.41 = (bf16[1,64,2,352]{3,2,1,0:T(2,128)(2,1)S(1)}, bf16[1,64,2,352]{3,2,1,0:T(2,128)(2,1)}, u32[]{:S(2)}) copy-start(bf16[1,64,2,352]{3,2,1,0:T(2,128)(2,1)} %param.27) | copy-start | bytes 270340
  36.9 9.1 %copy-start.43 = (bf16[1,352,64]{1,2,0:T(8,128)(2,1)S(1)}, bf16[1,352,64]{1,2,0:T(8,128)(2,1)}, u32[]{:S(2)}) copy-start(bf16[1,352,64]{1,2,0:T(8,128)(2,1)} %param.28) | copy-start | bytes 135172
  36.9 9.1 %copy-start.45 = (bf16[1,1,256,64]{2,3,1,0:T(8,128)(2,1)S(1)}, bf16[1,1,256,64]{2,3,1,0:T(8,128)(2,1)}, u32[]{:S(2)}) copy-start(bf16[1,1,256,64]{2,3,1,0:T(8,128)(2,1)} %param.25) | copy-start | bytes 98308
  36.9 9.2 %copy-start.48 = (f32[1,4,1,256]{3,2,1,0:T(1,128)S(1)}, f32[1,4,1,256]{3,2,1,0:T(1,128)}, u32[]{:S(2)}) copy-start(f32[1,4,1,256]{3,2,1,0:T(1,128)} %param.20) | copy-start | bytes 12292
  36.9 9.2 %copy-start.49 = (f32[1,4,1,256]{3,2,1,0:T(1,128)S(1)}, f32[1,4,1,256]{3,2,1,0:T(1,128)}, u32[]{:S(2)}) copy-start(f32[1,4,1,256]{3,2,1,0:T(1,128)} %param.21) | copy-start | bytes 12292
  36.9 33.6 %all-to-all-start = ((bf16[8,128,1024]{2,1,0:T(8,128)(2,1)}), bf16[8,128,1024]{2,1,0:T(8,128)(2,1)S(1)}, u32[]{:S(2)}, u32[]{:S(2)}) async-start(bf16[8,128,1024]{2,1,0:T(8,128)(2,1)} %broadcast_in_dim.106), calls=%async_computation | async-start | bytes 4194304 | tf_op jit(solution)/shard_map/all_to_all | solution.py:275
  70.6 9.4 %copy-start.19 = (bf16[8,128,1024]{2,1,0:T(8,128)(2,1)}, bf16[8,128,1024]{2,1,0:T(8,128)(2,1)S(1)}, u32[]{:S(2)}) copy-start(bf16[8,128,1024]{2,1,0:T(8,128)(2,1)S(1)} %all-to-all-done) | copy-start | bytes 6291460
  72.7 43.5 %all-to-all-start.2 = ((bf16[16,64,1312]{2,1,0:T(8,128)(2,1)}), bf16[16,64,1312]{2,1,0:T(8,128)(2,1)}, u32[]{:S(2)}, u32[]{:S(2)}) async-start(bf16[16,64,1312]{2,1,0:T(8,128)(2,1)} %broadcast_in_dim.112), calls=%async_computation.2 | async-start | bytes 5767168 | tf_op jit(solution)/shard_map/all_to_all | solution.py:275
  78.1 1.9 copy-start.32
  80.0 1.3 copy-start.27
  81.3 32.4 %copy-start.22 = (f32[1024,512]{1,0:T(8,128)}, f32[1024,512]{1,0:T(8,128)S(1)}, u32[]{:S(2)}) copy-start(f32[1024,512]{1,0:T(8,128)S(1)} %fusion.10) | copy-start | bytes 6291460
  83.0 4.5 copy-start.7
  83.0 2.3 copy-start.20
  83.1 4.8 copy-start.15
  86.0 0.8 copy-start.13
  90.2 23.4 %copy-start.47 = (f32[1,256]{1,0:T(1,128)S(1)}, f32[1,256]{1,0:T(1,128)}, u32[]{:S(2)}) copy-start(f32[1,256]{1,0:T(1,128)} %param.24) | copy-start | bytes 3076
  110.1 1.0 copy-start
  111.0 0.8 copy-start.1
  112.6 0.8 copy-start.5
  118.1 31.3 %copy-start.33 = (bf16[1,128,1024]{2,1,0:T(8,128)(2,1)S(1)}, bf16[1,128,1024]{2,1,0:T(8,128)(2,1)}, u32[]{:S(2)}) copy-start(bf16[1,128,1024]{2,1,0:T(8,128)(2,1)} %param.29) | copy-start | bytes 786436
  151.0 30.1 %all-to-all-start.6 = ((bf16[8,128,1024]{2,1,0:T(8,128)(2,1)}), bf16[8,128,1024]{2,1,0:T(8,128)(2,1)}, u32[]{:S(2)}, u32[]{:S(2)}) async-start(bf16[8,128,1024]{2,1,0:T(8,128)(2,1)} %broadcast_in_dim.114), calls=%async_computation.6 | async-start | bytes 4194304 | tf_op jit(solution)/shard_map/all_to_all | solution.py:275
  155.4 2.8 copy-start.42
  157.4 0.8 copy-start.9
  183.7 31.9 %all-to-all-start.4 = ((bf16[8,128,1024]{1,2,0:T(8,128)(2,1)}), bf16[8,128,1024]{1,2,0:T(8,128)(2,1)}, u32[]{:S(2)}, u32[]{:S(2)}) async-start(bf16[8,128,1024]{1,2,0:T(8,128)(2,1)} %broadcast_in_dim.113), calls=%async_computation.4 | async-start | bytes 4194304 | tf_op jit(solution)/shard_map/all_to_all | solution.py:275
  219.4 3.3 copy-start.24
  219.4 3.3 copy-start.52
  226.4 3.8 copy-start.54
  226.4 3.8 copy-start.55
  262.3 1.0 copy-start.10
  262.3 1.8 copy-start.34
  263.3 0.8 copy-start.17
  264.1 5.2 copy-start.50
  269.3 30.2 %all-to-all-start.8 = ((bf16[8,128,1024]{1,2,0:T(8,128)(2,1)}), bf16[8,128,1024]{1,2,0:T(8,128)(2,1)}, u32[]{:S(2)}, u32[]{:S(2)}) async-start(bf16[8,128,1024]{1,2,0:T(8,128)(2,1)} %broadcast_in_dim.117), calls=%async_computation.8 | async-start | bytes 4194304 | tf_op jit(solution)/shard_map/all_to_all | solution.py:275
  299.5 59.5 %all-to-all-start.5 = ((bf16[8,128,1024]{2,1,0:T(8,128)(2,1)}), bf16[8,128,1024]{2,1,0:T(8,128)(2,1)}, u32[]{:S(2)}, u32[]{:S(2)}) async-start(bf16[8,128,1024]{2,1,0:T(8,128)(2,1)} %bitcast.160), calls=%async_computation.5 | async-start | bytes 4194304 | tf_op jit(solution)/shard_map/all_to_all | solution.py:282
  309.0 4.0 copy-start.23
  313.0 1.4 copy-start.2
  313.0 1.4 copy-start.4
  313.0 1.4 copy-start.6
  314.4 27.3 %copy-start.8 = (f32[1024,256]{1,0:T(8,128)S(1)}, f32[1024,256]{1,0:T(8,128)}, u32[]{:S(2)}) copy-start(f32[1024,256]{1,0:T(8,128)} %copy-done.7) | copy-start | bytes 3145732
  342.0 1.2 copy-start.28
  342.0 1.5 copy-start.29
  344.5 1.0 copy-start.14
  346.4 3.9 copy-start.39
  346.4 1.3 copy-start.16
  346.5 1.8 copy-start.30
  346.5 2.1 copy-start.37
  346.8 3.5 copy-start.38
  350.2 2.0 copy-start.21
  350.4 1.0 copy-start.35
  359.0 5.7 %copy-start.36 = (bf16[1024,512]{1,0:T(8,128)(2,1)S(1)}, bf16[1024,512]{1,0:T(8,128)(2,1)}, u32[]{:S(2)}) copy-start(bf16[1024,512]{1,0:T(8,128)(2,1)} %copy-done.35) | copy-start | bytes 3145732
  359.0 5.8 %copy-start.40 = (bf16[1024,2]{1,0:T(8,128)(2,1)S(1)}, bf16[1024,2]{1,0:T(8,128)(2,1)}, u32[]{:S(2)}) copy-start(bf16[1024,2]{1,0:T(8,128)(2,1)} %copy-done.39) | copy-start | bytes 12292
  359.0 30.1 %all-to-all-start.10 = ((bf16[16,64,770]{2,1,0:T(8,128)(2,1)}), bf16[16,64,770]{2,1,0:T(8,128)(2,1)S(1)}, u32[]{:S(2)}, u32[]{:S(2)}) async-start(bf16[16,64,770]{2,1,0:T(8,128)(2,1)} %bitcast.153), calls=%async_computation.10 | async-start | bytes 3670016 | tf_op jit(solution)/shard_map/all_to_all | solution.py:282
  389.1 1.3 copy-start.25
  389.1 9.1 %copy-start.53 = (bf16[1024,352]{0,1:T(8,128)(2,1)S(1)}, bf16[1024,352]{0,1:T(8,128)(2,1)}, u32[]{:S(2)}) copy-start(bf16[1024,352]{0,1:T(8,128)(2,1)} %get-tuple-element.72) | copy-start | bytes 2162692
  390.4 34.0 %all-to-all-start.9 = ((bf16[8,128,1024]{2,1,0:T(8,128)(2,1)}), bf16[8,128,1024]{2,1,0:T(8,128)(2,1)S(1)}, u32[]{:S(2)}, u32[]{:S(2)}) async-start(bf16[8,128,1024]{2,1,0:T(8,128)(2,1)} %bitcast.161), calls=%async_computation.9 | async-start | bytes 4194304 | tf_op jit(solution)/shard_map/all_to_all | solution.py:282
  424.4 142.8 %all-to-all-start.11 = ((bf16[16,64,1312]{2,1,0:T(8,128)(2,1)}), bf16[16,64,1312]{2,1,0:T(8,128)(2,1)}, u32[]{:S(2)}, u32[]{:S(2)}) async-start(bf16[16,64,1312]{2,1,0:T(8,128)(2,1)} %concatenate.28), calls=%async_computation.11 | async-start | bytes 5767168 | tf_op jit(solution)/shard_map/all_to_all | solution.py:282
  491.2 73.4 %copy-start.11 = (f32[128,1024]{1,0:T(8,128)S(1)}, f32[128,1024]{1,0:T(8,128)}, u32[]{:S(2)}) copy-start(f32[128,1024]{1,0:T(8,128)} %copy-done.9) | copy-start | bytes 1572868
  491.2 73.4 %copy-start.18 = (f32[128,1024]{1,0:T(8,128)S(1)}, f32[128,1024]{1,0:T(8,128)}, u32[]{:S(2)}) copy-start(f32[128,1024]{1,0:T(8,128)} %copy-done.17) | copy-start | bytes 1572868
  495.3 0.8 copy-start.26
  (2 other events, 1.3 us)

commit v2 on v1

v2 whole, which is shorter than its diff:
```python
import functools

import jax
import jax.numpy as jnp
from jax import lax
from jax.experimental import pallas as pl
from jax.experimental.pallas import tpu as pltpu
from jax.sharding import Mesh
from jax.sharding import PartitionSpec as P
C = 128
F32 = jnp.float32
BF = jnp.bfloat16
EPS = 1e-06
GATED_EPS = 1e-05
AXES = ("ylo", "x", "core", "yhi", "z")
MESH_ID = pl.DeviceIdType.MESH
ROWS = 128
HALF = 64


class Place:
    def __init__(self):
        self.ylo, self.x, self.core, self.yhi, self.z = (lax.axis_index(a) for a in AXES)
        self.same = self.core == self.yhi
        self.block = self.core * 4 + self.z

    def at(self, **other):
        return {a: other.get(a, getattr(self, a)) for a in AXES}

    def sibling(self):
        return self.at(core=1 - self.core)

    def right(self):
        return self.at(z=lax.rem(self.z + 1, 4))

    def left(self):
        return self.at(z=lax.rem(self.z + 3, 4))

    def swapped(self):
        return self.at(core=self.yhi, yhi=self.core)

    def plane(self, i, j, m, flip):
        core, yhi = self.yhi, self.core
        if m and flip == "yhi":
            yhi = 1 - yhi
        if m and flip == "core":
            core = 1 - core
        return self.at(ylo=lax.rem(self.ylo + i, 2), x=lax.rem(self.x + j, 4), core=core, yhi=yhi)


OFFSETS = [(i, j, m) for i in range(2) for j in range(4) for m in range(2)]


def greet(place, ring, plane_sources, tensor_peers=False):
    bar = pltpu.get_barrier_semaphore()
    count = 0

    def say(device):
        pl.semaphore_signal(bar, inc=1, device_id=device, device_id_type=MESH_ID)

    if ring:
        for device in (place.sibling(), place.right(), place.left()):
            say(device)
        count += 3
    if tensor_peers:
        for device in peers_of(place):
            say(device)
        count += 7
    if plane_sources:
        for flip in plane_sources:
            for i, j, m in OFFSETS[1:]:
                say(place.plane(i, j, m, flip))
            count += 15

        @pl.when(jnp.logical_not(place.same))
        def _():
            say(place.swapped())

        count = count + jnp.where(place.same, 0, 1)
    pl.semaphore_wait(bar, count)


def remote(src, dst, sems, i, device):
    return pltpu.make_async_remote_copy(
        src_ref=src, dst_ref=dst, send_sem=sems.at[0, i], recv_sem=sems.at[1, i], device_id=device, device_id_type=MESH_ID
    )


class Swap:
    def __init__(self, place, src, dst, sems, i):
        self.place = place
        self.copy = remote(src, dst, sems, i, place.swapped())
        self.own = pltpu.make_async_copy(src, dst, sems.at[0, i])

    def start(self):
        pl.when(self.place.same)(self.own.start)
        pl.when(jnp.logical_not(self.place.same))(self.copy.start)

    def wait(self):
        pl.when(self.place.same)(self.own.wait)
        pl.when(jnp.logical_not(self.place.same))(self.copy.wait)


class Plane:
    def __init__(self, place, gather, src, dst, sems):
        self.place = place
        flip = "yhi" if gather else "core"
        mine = (place.ylo * 4 + place.x) * 2 + (place.core if gather else place.yhi)
        self.copies, self.arrivals = [], []
        for n, (i, j, m) in enumerate(OFFSETS):
            target = place.plane(i, j, m, flip)
            index = (target["ylo"] * 4 + target["x"]) * 2 + target["core"]
            part = src if gather else src.at[index]
            copy = pltpu.make_async_remote_copy(
                src_ref=part, dst_ref=dst.at[mine], send_sem=sems.at[0, n], recv_sem=sems.at[1, mine],
                device_id=target, device_id_type=MESH_ID,
            )
            other = place.yhi if gather else place.core
            slot = (lax.rem(place.ylo + i, 2) * 4 + lax.rem(place.x + j, 4)) * 2 + lax.rem(other + m, 2)
            arrival = pltpu.make_async_remote_copy(
                src_ref=part, dst_ref=dst.at[slot], send_sem=sems.at[0, n], recv_sem=sems.at[1, slot],
                device_id=target, device_id_type=MESH_ID,
            )
            self.copies.append(copy)
            self.arrivals.append(arrival)
            if n == 0:
                self.own = pltpu.make_async_copy(part, dst.at[mine], sems.at[0, 0])

    def start(self):
        pl.when(self.place.same)(self.own.start)
        pl.when(jnp.logical_not(self.place.same))(self.copies[0].start)
        for copy in self.copies[1:]:
            copy.start()

    def wait(self):
        pl.when(self.place.same)(self.own.wait)

        @pl.when(jnp.logical_not(self.place.same))
        def _():
            self.copies[0].wait_send()
            self.arrivals[0].wait_recv()

        for copy, arrival in zip(self.copies[1:], self.arrivals[1:]):
            copy.wait_send()
            arrival.wait_recv()


class Gather:
    def __init__(self, place, own, full, sems):
        p = self.place = place

        def rows(z, lo=0, n=ROWS):
            return full.at[pl.ds(pl.multiple_of((p.core * 4 + lax.rem(z, 4)) * ROWS + lo, HALF), n)]

        here, left, right = rows(p.z), rows(p.z + 3), rows(p.z + 1)
        far_lo, far_hi = rows(p.z + 2, 0, HALF), rows(p.z + 2, HALF, HALF)
        left_lo, right_hi = rows(p.z + 3, 0, HALF), rows(p.z + 1, HALF, HALF)
        sib = p.sibling()
        self.keep = pltpu.make_async_copy(own, here, sems.at[0, 9])
        self.c = [
            remote(own, here, sems, 0, p.right()),
            remote(own, here, sems, 1, p.left()),
            remote(own, here, sems, 2, sib),
            remote(left_lo, left_lo, sems, 3, p.right()),
            remote(right_hi, right_hi, sems, 4, p.left()),
            remote(left, left, sems, 5, sib),
            remote(right, right, sems, 6, sib),
            remote(far_lo, far_lo, sems, 7, sib),
            remote(far_hi, far_hi, sems, 8, sib),
        ]

    def start(self):
        self.keep.start()
        for i in (0, 1, 2):
            self.c[i].start()

    def middle(self):
        self.c[0].wait_recv()
        self.c[3].start()
        self.c[1].wait_recv()
        self.c[4].start()
        self.c[5].start()
        self.c[6].start()

    def late(self):
        self.c[3].wait_recv()
        self.c[7].start()
        self.c[4].wait_recv()
        self.c[8].start()

    def finish(self):
        self.keep.wait()
        for i in (0, 1, 3, 4):
            self.c[i].wait_send()
        for i in (2, 5, 6, 7, 8):
            self.c[i].wait()

    def run(self):
        self.start()
        self.middle()
        self.late()
        self.finish()


class Scatter:
    def __init__(self, place, terms, scratch, sems):
        p = self.place = place
        self.here, self.there, self.out, self.near, self.ends = scratch
        z = p.z
        self.order = [lax.rem(z + 2, 4), lax.rem(z + 1, 4), lax.rem(z + 3, 4), z]

        def rows(core, zz):
            return terms.at[pl.ds(pl.multiple_of((core * 4 + zz) * ROWS, ROWS), ROWS)]

        sib, right, left = p.sibling(), p.right(), p.left()
        self.cross, self.load = [], []
        for n, zz in enumerate(self.order):
            self.cross.append(remote(rows(1 - p.core, zz), self.there.at[n], sems, n, sib))
            self.load.append(pltpu.make_async_copy(rows(p.core, zz), self.here.at[n], sems.at[0, 10 + n]))
        lo, hi = pl.ds(0, HALF), pl.ds(HALF, HALF)
        out, near, ends = self.out, self.near, self.ends
        self.far_lo = remote(out.at[0, lo], near.at[0], sems, 4, right)
        self.far_hi = remote(out.at[0, hi], near.at[1], sems, 5, left)
        self.right_hi = remote(out.at[1, hi], ends.at[0, hi], sems, 6, right)
        self.left_lo = remote(out.at[2, lo], ends.at[1, lo], sems, 7, left)
        self.right_lo = remote(out.at[1, lo], ends.at[0, lo], sems, 8, right)
        self.left_hi = remote(out.at[2, hi], ends.at[1, hi], sems, 9, left)

    def start(self):
        for a, b in zip(self.cross, self.load):
            a.start()
            b.start()

    def pair(self, n, rows=slice(None)):
        return self.here[n, rows].astype(F32) + self.there[n, rows].astype(F32)

    def arrived(self, n):
        self.load[n].wait()
        self.cross[n].wait()

    def middle(self):
        self.arrived(0)
        self.out[0] = self.pair(0).astype(BF)
        self.far_lo.start()
        self.far_hi.start()
        lo, hi = slice(0, HALF), slice(HALF, ROWS)
        self.arrived(1)
        self.out[1, hi] = self.pair(1, hi).astype(BF)
        self.right_hi.start()
        self.arrived(2)
        self.out[2, lo] = self.pair(2, lo).astype(BF)
        self.left_lo.start()
        self.arrived(3)

    def late(self):
        lo, hi = slice(0, HALF), slice(HALF, ROWS)
        self.far_lo.wait_recv()
        self.out[1, lo] = (self.pair(1, lo) + self.near[0].astype(F32)).astype(BF)
        self.right_lo.start()
        self.far_hi.wait_recv()
        self.out[2, hi] = (self.pair(2, hi) + self.near[1].astype(F32)).astype(BF)
        self.left_hi.start()

    def finish(self):
        for c in (self.right_hi, self.left_lo, self.right_lo, self.left_hi):
            c.wait()
        self.far_lo.wait_send()
        self.far_hi.wait_send()
        return self.pair(3) + self.ends[0].astype(F32) + self.ends[1].astype(F32)

    def run(self):
        self.start()
        self.middle()
        self.late()
        return self.finish()


def scatter_scratch(d):
    return [
        pltpu.VMEM((4, ROWS, d), BF),
        pltpu.VMEM((4, ROWS, d), BF),
        pltpu.VMEM((3, ROWS, d), BF),
        pltpu.VMEM((2, HALF, d), BF),
        pltpu.VMEM((2, ROWS, d), BF),
    ]


GATHER_SEMS = pltpu.SemaphoreType.DMA((2, 10))
SCATTER_SEMS = pltpu.SemaphoreType.DMA((2, 14))
PLANE_SEMS = pltpu.SemaphoreType.DMA((2, 16))


def peers_of(place):
    return [
        place.at(yhi=lax.rem(place.yhi + i, 2), z=lax.rem(place.z + j, 4)) for i in range(2) for j in range(4) if i or j
    ]


def normed(x, gain):
    return x * lax.rsqrt(jnp.mean(x * x, -1, keepdims=True) + EPS) * gain


def norm_back(x, gain, grad):
    r = lax.rsqrt(jnp.mean(x * x, -1, keepdims=True) + EPS)
    weighted = gain * grad
    by_x = r * weighted - x * (r * r * r) * jnp.mean(x * weighted, -1, keepdims=True)
    return by_x, jnp.sum(grad * x * r, 0, keepdims=True)


def entry_kernel(x_ref, g_ref, gain_ref, head_ref, w_ref, xs_ref, gs_ref, heads_ref, wall_ref, rows_ref,
                 own, sw_sems, pl_sems, ga_sems):
    place = Place()
    greet(place, True, ("core",))
    swaps = [Swap(place, a, b, sw_sems, i) for i, (a, b) in enumerate(((x_ref, xs_ref), (g_ref, gs_ref), (head_ref, heads_ref)))]
    weights = Plane(place, True, w_ref, wall_ref, pl_sems)
    swaps[0].start()
    swaps[2].start()
    weights.start()
    swaps[1].start()
    swaps[0].wait()
    own[...] = normed(xs_ref[...].astype(F32), gain_ref[...]).astype(BF)
    Gather(place, own, rows_ref, ga_sems).run()
    swaps[1].wait()
    swaps[2].wait()
    weights.wait()


def sum_norm_gather_kernel(terms_ref, x_ref, gain_ref, stream_ref, rows_ref, own, here, there, out, near, ends, sc_sems, ga_sems):
    place = Place()
    greet(place, True, ())
    stream = x_ref[...].astype(F32) + Scatter(place, terms_ref, (here, there, out, near, ends), sc_sems).run()
    stream_ref[...] = stream
    own[...] = normed(stream, gain_ref[...]).astype(BF)
    Gather(place, own, rows_ref, ga_sems).run()


def sum_back_gather_kernel(terms_ref, stream_ref, gain_ref, g_ref, grad_ref, dgain_ref, rows_ref, own, here, there, out,
                           near, ends, sc_sems, ga_sems):
    place = Place()
    greet(place, True, ())
    grad = Scatter(place, terms_ref, (here, there, out, near, ends), sc_sems).run()
    by_x, by_gain = norm_back(stream_ref[...], gain_ref[...], grad)
    grad = g_ref[...].astype(F32) + by_x
    grad_ref[...] = grad
    own[...] = grad.astype(BF)
    ring = Gather(place, own, rows_ref, ga_sems)
    ring.start()
    dgain_ref[...] = by_gain
    ring.middle()
    ring.late()
    ring.finish()


def exit_kernel(terms_ref, x_ref, gain_ref, grad_ref, output_ref, dw_ref, small_ref, final_ref, input_ref, parts_ref, sums_ref,
                own, here, there, out, near, ends, mine, plane_sums, total, peer_sums, sc_sems, sw_sems, pl_sems, sm_sems, pe_sems):
    place = Place()
    greet(place, True, ("yhi",), True)
    d = gain_ref.shape[1]
    swap_output = Swap(place, output_ref, final_ref, sw_sems, 0)
    swap_output.start()
    ring = Scatter(place, terms_ref, (here, there, out, near, ends), sc_sems)
    ring.start()
    weights = Plane(place, False, dw_ref, parts_ref, pl_sems)
    weights.start()
    ring.middle()
    ring.late()
    grad = ring.finish()
    by_x, by_gain = norm_back(x_ref[...].astype(F32), gain_ref[...], grad)
    own[...] = (grad_ref[...] + by_x).astype(BF)
    swap_input = Swap(place, own, input_ref, sw_sems, 1)
    swap_input.start()
    mine[...] = small_ref[...]
    for i in range(d // 128):
        mine[i : i + 1, :] = by_gain[:, i * 128 : (i + 1) * 128]
    small = PlaneSame(place, mine, plane_sums, sm_sems)
    small.start()
    small.wait()
    subtotal = plane_sums[0]
    for i in range(1, 16):
        subtotal = subtotal + plane_sums[i]
    total[...] = subtotal
    n = peer_sums.shape[1]
    copies = [
        remote(total.at[pl.ds(0, n)], peer_sums.at[i], pe_sems, i, device) for i, device in enumerate(peers_of(place))
    ]
    for copy in copies:
        copy.start()
    sums_ref[...] = subtotal
    for copy in copies:
        copy.wait()
    gains = subtotal[:n]
    for i in range(7):
        gains = gains + peer_sums[i]
    sums_ref[0:n, :] = gains
    weights.wait()
    swap_output.wait()
    swap_input.wait()


class PlaneSame(Plane):
    def __init__(self, place, src, dst, sems):
        Plane.__init__(self, place, False, Same(src), dst, sems)


class Same:
    def __init__(self, ref):
        self.ref = ref
        self.at = self

    def __getitem__(self, index):
        return self.ref


HI = lax.Precision.HIGHEST
LO = lax.Precision.DEFAULT
NN = (((1,), (0,)), ((), ()))
NT = (((1,), (1,)), ((), ()))
TN = (((0,), (0,)), ((), ()))


def mm(a, b, dims=NN, precision=HI):
    return lax.dot_general(a, b, dims, precision=precision, preferred_element_type=F32)


def chunk_masks():
    row = lax.broadcasted_iota(jnp.int32, (C, C), 0)
    col = lax.broadcasted_iota(jnp.int32, (C, C), 1)
    return row, col


def decay_parts(g, row, col):
    lower = (row >= col).astype(F32)
    cum = mm(lower, g)
    table = jnp.where(row >= col, jnp.exp(jnp.where(row >= col, cum - cum.T, 0.0)), 0.0)
    last = cum[C - 1 : C, :]
    return table, jnp.exp(cum), jnp.exp(last - cum), jnp.exp(last)


def wide(x):
    return jnp.concatenate([x, x], axis=1)


def inverse_many(systems, row, col, prec):
    eye = (row == col).astype(F32)
    near = (row // 8) == (col // 8)
    a1 = [jnp.where(near, a, 0.0) for a in systems]
    a2 = [mm(a, a, precision=prec) for a in a1]
    x = [eye - a for a in a1]
    a4 = [mm(a, a, precision=prec) for a in a2]
    x = [y + mm(y, a, precision=prec) for y, a in zip(x, a2)]
    x = [y + mm(y, a, precision=prec) for y, a in zip(x, a4)]
    size = 8
    while size < C:
        pick = ((row // (2 * size)) == (col // (2 * size))) & ((row // size) != (col // size))
        off = [jnp.where(pick, a, 0.0) for a in systems]
        y = [mm(o, t, precision=prec) for o, t in zip(off, x)]
        x = [t - mm(t, z, precision=prec) for t, z in zip(x, y)]
        size *= 2
    return x


def fwd_kernel(P_, group, q_ref, k_ref, v_ref, b_ref, g_ref, grow_ref, shard_ref, o_ref, t_ref, u_ref, s_ref, f_ref, w_ref,
               grows_ref, wall_ref, z_ref, pl_sems, ga_sems):
    place = Place()
    greet(place, True, ("core",))
    weights = Plane(place, True, shard_ref, wall_ref, pl_sems)
    ring = Gather(place, grow_ref, grows_ref, ga_sems)
    weights.start()
    ring.start()
    nb = q_ref.shape[0] // C
    row, col = chunk_masks()

    def first(i, _):
        cs = [pl.ds(pl.multiple_of((i * group + j) * C, C), C) for j in range(group)]
        q = [q_ref[c, :] for c in cs]
        k = [k_ref[c, :] for c in cs]
        v = [v_ref[c, :] for c in cs]
        b = [b_ref[c, :] for c in cs]
        parts = [decay_parts(g_ref[c, :], row, col) for c in cs]
        kk = [mm(x, x, NT, P_["kk"]) for x in k]
        system = [jnp.where(row > col, bb * x * p[0], 0.0) for bb, x, p in zip(b, kk, parts)]
        t = inverse_many(system, row, col, P_["inv"])
        w = [mm(tt, bb * p[1] * x, precision=P_["w"]) for tt, bb, p, x in zip(t, b, parts, k)]
        u0 = [mm(tt, wide(bb) * x, precision=P_["u"]) for tt, bb, x in zip(t, b, v)]
        kd = [x * p[2] for x, p in zip(k, parts)]
        eye = (row == col).astype(F32)
        for c, kdd, ww, uu, tt, p in zip(cs, kd, w, u0, t, parts):
            t_ref[c, :] = tt
            w_ref[c, :] = ww
            u_ref[c, :] = uu
            f_ref[c, :] = eye * p[3] - mm(kdd, ww, TN, P_["f"])
            z_ref[c, :] = mm(kdd, uu, TN, P_["z"])
        return 0

    lax.fori_loop(0, nb // group, first, 0)
    ring.middle()
    state = jnp.zeros((C, v_ref.shape[1]), F32)
    for i in range(nb):
        c = pl.ds(i * C, C)
        s_ref[c, :] = state
        if i < nb - 1:
            state = z_ref[c, :] + mm(f_ref[c, :], state, precision=P_["chain"])
    ring.late()

    def last(i, _):
        cs = [pl.ds(pl.multiple_of((i * group + j) * C, C), C) for j in range(group)]
        for c in cs:
            q, k, s = q_ref[c, :], k_ref[c, :], s_ref[c, :]
            table, scale, _, _ = decay_parts(g_ref[c, :], row, col)
            u = u_ref[c, :] - mm(w_ref[c, :], s, precision=P_["ws"])
            u_ref[c, :] = u
            scores = mm(q, k, NT, P_["qk"]) * table
            o_ref[c, :] = mm(q * scale, s, precision=P_["o"]) + mm(scores, u, precision=P_["o"])
        return 0

    lax.fori_loop(0, nb // group, last, 0)
    ring.finish()
    weights.wait()


def bwd_kernel(P_, group, q_ref, k_ref, v_ref, b_ref, g_ref, t_ref, u_ref, s_ref, f_ref, w_ref, do_ref,
               terms_ref, stream_ref, dw_ref, dq_ref, dk_ref, dv_ref, db_ref, dg_ref, output_ref, parts_ref, ds_ref, x_ref,
               here, there, out, near, ends, sc_sems, pl_sems):
    place = Place()
    greet(place, True, ("yhi",))
    ring = Scatter(place, terms_ref, (here, there, out, near, ends), sc_sems)
    weights = Plane(place, False, dw_ref, parts_ref, pl_sems)
    ring.start()
    weights.start()
    nb = q_ref.shape[0] // C
    row, col = chunk_masks()

    def first(i, _):
        cs = [pl.ds(pl.multiple_of((i * group + j) * C, C), C) for j in range(group)]
        for c in cs:
            q, k, do = q_ref[c, :], k_ref[c, :], do_ref[c, :]
            table, scale, _, _ = decay_parts(g_ref[c, :], row, col)
            scores = mm(q, k, NT, P_["qk"]) * table
            x = mm(scores, do, TN, P_["bx"])
            x_ref[c, :] = x
            ds_ref[c, :] = mm(q * scale, do, TN, P_["bx"]) - mm(w_ref[c, :], x, TN, P_["bx"])
        return 0

    lax.fori_loop(0, nb // group, first, 0)
    ring.middle()
    carry = jnp.zeros((C, v_ref.shape[1]), F32)
    for i in reversed(range(nb)):
        c = pl.ds(i * C, C)
        own = ds_ref[c, :]
        ds_ref[c, :] = carry
        if i > 0:
            carry = own + mm(f_ref[c, :], carry, TN, P_["chain"])
    ring.late()

    def last(i, _):
        cs = [pl.ds(pl.multiple_of((i * group + j) * C, C), C) for j in range(group)]
        for c in cs:
            q, k, v, b, do = q_ref[c, :], k_ref[c, :], v_ref[c, :], b_ref[c, :], do_ref[c, :]
            t, u, s, ds = t_ref[c, :], u_ref[c, :], s_ref[c, :], ds_ref[c, :]
            table, scale, tail, total = decay_parts(g_ref[c, :], row, col)
            p = P_["bl"]
            qk = mm(q, k, NT, p)
            kk = mm(k, k, NT, p)
            ks = mm(k, s, precision=p)
            qs = mm(q, s, precision=p)
            kd = k * tail
            du = x_ref[c, :] + mm(kd, ds, precision=p)
            dr = mm(t, du, TN, P_["bt"])
            dp = jnp.where(row >= col, mm(do, u, NT, p), 0.0)
            da = jnp.where(row > col, -mm(dr, u, NT, p), 0.0)
            dqk = dp * table
            dkk = da * b * table
            n = dqk * qk + dkk * kk
            dkd = mm(u, ds, NT, p)
            dq_ref[c, :] = scale * mm(do, s, NT, p) + mm(dqk, k, precision=p)
            bdr = wide(b) * dr
            dk_ref[c, :] = (
                mm(dqk, q, TN, p)
                + mm(dkk, k, precision=p)
                + mm(dkk, k, TN, p)
                + dkd * tail
                - scale * mm(bdr, s, NT, p)
            )
            dv_ref[c, :] = bdr
            sc2 = wide(scale)
            db = jnp.sum(dr * (v - sc2 * ks), 1, keepdims=True) + jnp.sum(da * table * kk, 1, keepdims=True)
            db_ref[c, :] = jnp.broadcast_to(db, (C, C))
            tails = jnp.sum(dkd * kd, 1, keepdims=True)
            dcum = (
                jnp.sum(n, 1, keepdims=True)
                - jnp.sum(n.T, 1, keepdims=True)
                + jnp.sum(sc2 * (do * qs - bdr * ks), 1, keepdims=True)
                - tails
            )
            dcum = jnp.broadcast_to(dcum, (C, C))
            extra = jnp.sum(tails) + jnp.sum(ds * s * wide(jnp.broadcast_to(total, (C, C))))
            upper = (row <= col).astype(F32)
            dg_ref[c, :] = mm(upper, dcum) + extra
        return 0

    lax.fori_loop(0, nb // group, last, 0)
    output_ref[...] = (stream_ref[...] + ring.finish()).astype(BF)
    weights.wait()


KEYS = ("kk", "inv", "w", "u", "f", "z", "chain", "ws", "qk", "o", "bx", "bl", "bt")
PRECS = {key: HI for key in KEYS}
VM = pl.BlockSpec(memory_space=pltpu.VMEM)
ANY = pl.BlockSpec(memory_space=pl.ANY)


def call(kernel, name, number, ins, in_specs, outs, out_specs, scratch):
    return pl.pallas_call(
        kernel,
        name=name,
        out_shape=[jax.ShapeDtypeStruct(s, t) for s, t in outs],
        in_specs=in_specs,
        out_specs=out_specs,
        scratch_shapes=scratch,
        compiler_params=pltpu.CompilerParams(
            collective_id=number, has_side_effects=True, vmem_limit_bytes=48 * 2**20
        ),
    )(*ins)


def causal_conv(inputs, taps):
    length = inputs.shape[0]
    padded = jnp.pad(inputs, ((taps.shape[0] - 1, 0), (0, 0)))
    summed = padded[0:length] * taps[0]
    for shift_at in range(1, taps.shape[0]):
        summed = summed + padded[shift_at : shift_at + length] * taps[shift_at]
    return summed


def before_delta(qk_pre, v_pre, bd_pre, conv_qk, conv_v, decay_log, decay_bias):
    dk = qk_pre.shape[-1] // 2
    rows = jax.nn.silu(causal_conv(qk_pre, conv_qk))
    q, k = rows[:, :dk], rows[:, dk:]
    q = q * lax.rsqrt(jnp.sum(q * q, -1, keepdims=True) + EPS) * dk ** (-0.5)
    k = k * lax.rsqrt(jnp.sum(k * k, -1, keepdims=True) + EPS)
    v = jax.nn.silu(causal_conv(v_pre, conv_v))
    b = jax.nn.sigmoid(bd_pre[:, 0])
    g = -jnp.exp(decay_log) * jax.nn.softplus(bd_pre[:, 1] + decay_bias)
    return q, k, v, jnp.broadcast_to(b[:, None], (b.shape[0], C)), jnp.broadcast_to(g[:, None], (g.shape[0], C))


def after_delta(delta_out, gates, gain):
    r = lax.rsqrt(jnp.mean(delta_out * delta_out, -1, keepdims=True) + GATED_EPS)
    return delta_out * r * gain * jax.nn.silu(gates)


def dot(a, b, dims=NN):
    return lax.dot_general(a, b, dims, preferred_element_type=F32)


def padded(x, width):
    return jnp.pad(x, ((0, 0), (0, width - x.shape[1])))


def up_to(n, k):
    return -(-n // k) * k


def body(
    block_input,
    mixer_gain,
    query_key_weight,
    value_gate_weight,
    beta_decay_weight,
    conv_query_key,
    conv_value,
    decay_log,
    decay_bias,
    out_gain,
    out_weight,
    forward_gain,
    gate_up_weight,
    down_weight,
    out_cotangent,
):
    d = block_input.shape[2]
    n = block_input.shape[1] * 8
    nqk, nvg, nbd = query_key_weight.shape[-1], value_gate_weight.shape[-1], beta_decay_weight.shape[-1]
    ff = gate_up_weight.shape[-1]
    dv = out_weight.shape[2]
    own_d = query_key_weight.shape[1]
    wide_in, wide_rest = up_to(nqk + nvg + nbd, 128), up_to(dv + 3 * ff, 128)
    first_pack = padded(
        jnp.concatenate([query_key_weight[0, :, 0], value_gate_weight[0, :, 0], beta_decay_weight[0, :, 0]], 1), wide_in
    )
    second_pack = padded(
        jnp.concatenate([out_weight[0, 0].T, gate_up_weight[0].reshape(-1, 2 * ff), down_weight[0].T], 1), wide_rest
    )
    taps = conv_query_key.shape[1]
    heads = jnp.concatenate(
        [
            conv_query_key[0, :, 0].reshape(-1, 128),
            conv_value[0, :, 0].reshape(-1, 128),
            padded(jnp.concatenate([decay_log, decay_bias], 1), 128),
        ]
    )
    head_rows = up_to(heads.shape[0], 8)
    heads = jnp.pad(heads, ((0, head_rows - heads.shape[0]), (0, 0)))
    sems = pltpu.SemaphoreType.DMA
    block = (ROWS, d)

    x, g, heads, w_in, rows = call(
        entry_kernel,
        "entry_exchange",
        0,
        (block_input[0], out_cotangent[0], mixer_gain, heads, first_pack),
        [VM, VM, VM, VM, ANY],
        [(block, BF), (block, BF), (heads.shape, F32), ((16, own_d, wide_in), BF), ((n, d), BF)],
        [VM, VM, VM, ANY, ANY],
        [pltpu.VMEM(block, BF), sems((2, 3)), PLANE_SEMS, GATHER_SEMS],
    )
    w_in = w_in.reshape(d, wide_in)
    size = taps * nqk // 128
    conv_qk, conv_v = heads[:size].reshape(taps, nqk), heads[size : 2 * size].reshape(taps, dv)
    decays = heads[2 * size]

    pre = dot(rows, w_in)
    gates = pre[:, nqk + dv : nqk + nvg]
    (q, k, v, b, ld), pre_back = jax.vjp(
        before_delta, pre[:, :nqk], pre[:, nqk : nqk + dv], pre[:, nqk + nvg :], conv_qk, conv_v, decays[0], decays[1]
    )
    f = lambda width: ((n, width), F32)
    delta_out, t, u, s, fm, w, g_rows, w_rest = call(
        functools.partial(fwd_kernel, PRECS, 4),
        "delta_forward",
        1,
        (q, k, v, b, ld, g, second_pack),
        [VM] * 5 + [ANY] * 2,
        [f(dv), f(C), f(dv), f(dv), f(C), f(C), ((n, d), BF), ((16, own_d, wide_rest), BF)],
        [VM] * 6 + [ANY] * 2,
        [pltpu.VMEM((n, dv), F32), PLANE_SEMS, GATHER_SEMS],
    )
    w_rest = w_rest.reshape(d, wide_rest)
    w_out, w_gu, w_down = w_rest[:, :dv], w_rest[:, dv : dv + 2 * ff], w_rest[:, dv + 2 * ff : dv + 3 * ff]
    mixed, post_back = jax.vjp(after_delta, delta_out, gates, out_gain)
    mixed = mixed.astype(BF)
    stream, forward_rows = call(
        sum_norm_gather_kernel,
        "sum_norm_gather",
        2,
        (dot(mixed, w_out, NT).astype(BF), x, forward_gain),
        [ANY, VM, VM],
        [(block, F32), ((n, d), BF)],
        [VM, ANY],
        [pltpu.VMEM(block, BF)] + scatter_scratch(d) + [SCATTER_SEMS, GATHER_SEMS],
    )
    gate = dot(forward_rows, w_gu[:, :ff])
    up = dot(forward_rows, w_gu[:, ff:])
    sg = jax.nn.sigmoid(gate)
    hidden = (gate * sg * up).astype(BF)
    grad_hidden = dot(g_rows, w_down)
    grad_gu = jnp.concatenate(
        [(grad_hidden * up * sg * (1.0 + gate * (1.0 - sg))).astype(BF), (grad_hidden * gate * sg).astype(BF)], 1
    )
    grad_stream, grad_fgain, m_rows = call(
        sum_back_gather_kernel,
        "sum_back_gather",
        3,
        (dot(grad_gu, w_gu, NT).astype(BF), stream, forward_gain, g),
        [ANY, VM, VM, VM],
        [(block, F32), ((1, d), F32), ((n, d), BF)],
        [VM, VM, ANY],
        [pltpu.VMEM(block, BF)] + scatter_scratch(d) + [SCATTER_SEMS, GATHER_SEMS],
    )
    grad_rest = padded(
        jnp.concatenate([dot(m_rows, mixed, TN), dot(forward_rows, grad_gu, TN), dot(g_rows, hidden, TN)], 1).astype(BF),
        wide_rest,
    ).reshape(16, own_d, wide_rest)
    grad_delta, grad_gates, grad_ogain = post_back(dot(m_rows, w_out))
    dq, dk, dvalue, db, dg, output, rest_parts = call(
        functools.partial(bwd_kernel, PRECS, 2),
        "delta_backward",
        4,
        (q, k, v, b, ld, t, u, s, fm, w, grad_delta, dot(hidden, w_down, NT).astype(BF), stream, grad_rest),
        [VM] * 11 + [ANY, VM, ANY],
        [f(C), f(C), f(dv), f(C), f(C), (block, BF), ((16, own_d, wide_rest), BF)],
        [VM] * 6 + [ANY],
        [pltpu.VMEM((n, dv), F32)] * 2 + scatter_scratch(d) + [SCATTER_SEMS, PLANE_SEMS],
    )
    share = 1.0 / C
    d_qk, d_v, d_bd, grad_cqk, grad_cv, grad_dlog, grad_dbias = pre_back((dq, dk, dvalue, db * share, dg * share))
    d_in = padded(jnp.concatenate([d_qk, d_v, grad_gates, d_bd], 1).astype(BF), wide_in)
    gain_rows = up_to((2 * d + dv) // 128, 8)
    zero = jnp.zeros((1, 128), F32)
    small = jnp.concatenate(
        [
            jnp.zeros((d // 128, 128), F32),
            grad_fgain.reshape(-1, 128),
            grad_ogain.reshape(-1, 128),
            jnp.zeros((gain_rows - (2 * d + dv) // 128, 128), F32),
            grad_cqk.reshape(-1, 128),
            grad_cv.reshape(-1, 128),
            padded(jnp.stack([grad_dlog, grad_dbias])[None], 128),
            jnp.zeros((head_rows - 2 * size - 1, 128), F32),
        ]
    )
    small_rows = small.shape[0]
    final, input_grad, in_parts, sums = call(
        exit_kernel,
        "exit_exchange",
        5,
        (
            dot(d_in, w_in, NT).astype(BF),
            x,
            mixer_gain,
            grad_stream,
            output,
            dot(rows, d_in, TN).astype(BF).reshape(16, own_d, wide_in),
            small,
        ),
        [ANY, VM, VM, VM, VM, ANY, VM],
        [(block, BF), (block, BF), ((16, own_d, wide_in), BF), ((small_rows, 128), F32)],
        [ANY, ANY, ANY, VM],
        [pltpu.VMEM(block, BF)]
        + scatter_scratch(d)
        + [
            pltpu.VMEM((small_rows, 128), F32),
            pltpu.VMEM((16, small_rows, 128), F32),
            pltpu.VMEM((small_rows, 128), F32),
            pltpu.VMEM((7, gain_rows, 128), F32),
            SCATTER_SEMS,
            sems((2, 2)),
            PLANE_SEMS,
            PLANE_SEMS,
            sems((2, 7)),
        ],
    )
    own_rest = jnp.sum(rest_parts.astype(F32), 0)
    own_in = jnp.sum(in_parts.astype(F32), 0)
    k8 = d // 128
    hs = sums[gain_rows:]
    return (
        final.astype(F32)[None],
        input_grad.astype(F32)[None],
        sums[:k8].reshape(1, d),
        own_in[None, :, None, :nqk],
        own_in[None, :, None, nqk : nqk + nvg],
        own_in[None, :, None, nqk + nvg : nqk + nvg + nbd],
        hs[:size].reshape(1, taps, 1, nqk),
        hs[size : 2 * size].reshape(1, taps, 1, dv),
        hs[2 * size : 2 * size + 1, :1],
        hs[2 * size : 2 * size + 1, 1:2],
        sums[2 * k8 : 2 * k8 + dv // 128].reshape(1, dv),
        own_rest[:, :dv].T[None, None],
        sums[k8 : 2 * k8].reshape(1, d),
        own_rest[:, dv : dv + 2 * ff].reshape(1, -1, 2, ff),
        own_rest[:, dv + 2 * ff : dv + 3 * ff].T[None],
    )


def solution(mesh):
    parts = Mesh(mesh.devices.reshape(2, 4, 2, 2, 4), AXES)
    dp, tp = ("ylo", "x", "core"), ("yhi", "z")
    stream = P(dp, tp, None)
    head = P(None, tp)
    proj = P(None, dp, tp, None)
    conv = P(None, None, tp, None)
    out_w, gu_w, down_w = P(None, tp, None, dp), P(None, dp, None, tp), P(None, tp, dp)
    return jax.shard_map(
        body,
        mesh=parts,
        in_specs=(stream, P(), proj, proj, proj, conv, conv, head, head, P(), out_w, P(), gu_w, down_w, stream),
        out_specs=(stream, stream, P(), proj, proj, proj, conv, conv, head, head, P(), out_w, P(), gu_w, down_w),
        check_vma=False,
    )
```

time: 583 us -> 332 us (0.57)
  blocking collectives: 183 us -> 0 us
  Pallas kernels: 47.1 us -> 227 us
  waiting for transfers between devices: 132 us -> 0 us
  starting transfers between devices: 58.6 us -> 0 us
  local copies, waits for them, and re-layouts: 67.1 us -> 31.5 us
  matrix products: 49.1 us -> 29.7 us
    pallas_call x2 -> x6, Pallas kernels: 47.1 us -> 227 us  [call(): pl.pallas_call(kernel, name=name, out_shape=[jax.ShapeDtypeStruct(s, t) f...]
    all_to_all x10 -> x0, waiting for transfers between devices: 132 us -> none  [the longest x6 113 us: gather(): lax.all_to_all(copies, axis, split_axis=0, concat_axis=0, tiled=True)]
    psum x2 -> x0, blocking collectives: 119 us -> none  [the longest x1 65.1 us: body(): lax.psum(jnp.concatenate([grad_mgain, grad_fgain, grad_ogain]), (DP, TP))]
    all_to_all x2 -> x0, blocking collectives: 63.4 us -> none  [scatter_sum(): tiles = lax.all_to_all(tiles, axis, 0, 0, tiled=True)]
    all_to_all x10 -> x0, starting transfers between devices: 58.6 us -> none  [the longest x6 34.2 us: gather(): lax.all_to_all(copies, axis, split_axis=0, concat_axis=0, tiled=True)]
    dot_general x15 -> x13, matrix products: 49.1 us -> 29.7 us  [dot(): return lax.dot_general(a, b, dims, preferred_element_type=F32)]
    broadcast_in_dim x12 -> x8, local copies, waits for them, and re-layouts: 13.7 us -> 1.97 us  [the longest x1 0.73 us: body(): own_rest[:, dv + 2 * ff:dv + 3 * ff].T[None]]
    dot_general x3 -> x0, local copies, waits for them, and re-layouts: 9.37 us -> none  [dot(): return lax.dot_general(a, b, dims, preferred_element_type=F32)]
  transfers between devices with their start and end apart: 10 -> 0, of which waited for: 7 -> 0; matrix products, arithmetic and copies ran while one was open for 17% -> 0% of each run, Pallas kernels for 8% -> 0%
where the time goes in v2:
time: 332 us; the launch traced here: 327 us
  Pallas kernels  227 us (68%)
  other arithmetic  34 us (10%)
  local copies, waits for them, and re-layouts  31.5 us (9%)
  matrix products  29.7 us (9%)
  between operations  4.32 us (1%)
    pallas_call x6, Pallas kernels, call(): pl.pallas_call(kernel, name=name, out_shape=[jax.ShapeDtypeStruct(s, t) f...  227 us
    dot_general x13, matrix products, dot(): return lax.dot_general(a, b, dims, preferred_element_type=F32)  29.7 us
    unnamed x76, local copies, waits for them, and re-layouts  13.8 us

profile of v2, /device:TPU:1, one launch (start us, length us, event | category | flops | bytes accessed | tf_op | source)
XLA Modules:
  0.0 326.7 jit_solution(3118642196000366197)
XLA Ops:
  2.0 0.7 select_maximum_fusion.head_ref
  2.7 0.8 copy.46
  3.5 0.9 fusion.32.w_ref
  4.3 1.0 reshape_squeeze.11
  5.4 0.9 concatenate.29
  6.3 0.9 copy-done.13
  7.3 0.9 copy-done.14
  8.2 0.7 copy-done.16
  8.9 35.5 %entry_exchange.1 = (bf16[128,1024]{1,0:T(8,128)(2,1)S(1)}, bf16[128,1024]{1,0:T(8,128)(2,1)S(1)}, f32[24,128]{1,0:T(8,128)S(1)}, bf16[16,64,896]{2,1,0:T(8,128)(2,1)S(1)}, bf16[1024,1024]{1,0:T(8,128)(2,1)S(1)}) custom-call(bf16[128,1024]{1,0:T(8,128)(2,1)S(1)} %bitcast.90, bf16[128,1024]{1,0:T(8,128)(2,1)S(1)} %bitcast.91, f32[1,1024]{1,0:T(1,128)S(1)} %copy-done.16, ...), custom_call_target="tpu_custom_call" | custom-call | tf_op jit(solution)/shard_map/entry_exchange/pallas_call | solution.py:613
  44.4 1.2 copy-done.20
  45.6 0.7 fusion.52
  47.0 5.6 %fusion.53 = f32[1024,896]{1,0:T(8,128)} fusion(bf16[1024,1024]{1,0:T(8,128)(2,1)S(1)} %get-tuple-element.44, bf16[1024,896]{1,0:T(8,128)(2,1)} %bitcast.93), kind=kOutput, calls=%fused_computation.158 | convolution fusion | flops 1879048192 | bytes 7602176 | tf_op jit(solution)/shard_map/dot_general | solution.py:653
  52.6 2.2 fusion.48
  54.9 1.2 copy.61
  56.1 0.7 fusion.39
  57.0 1.1 copy.54
  58.3 1.7 fusion.49
  60.0 2.3 fusion.11
  63.3 47.6 %delta_forward.1 = (f32[1024,256]{1,0:T(8,128)S(1)}, f32[1024,128]{1,0:T(8,128)S(1)}, f32[1024,256]{1,0:T(8,128)S(1)}, f32[1024,256]{1,0:T(8,128)}, f32[1024,128...) custom-call(f32[1024,128]{1,0:T(8,128)S(1)} %get-tuple-element.169.q_ref, ...), custom_call_target="tpu_custom_call" | custom-call | tf_op jit(solution)/shard_map/delta_forward/pallas_call | solution.py:613
  111.2 2.6 multiply_convert_fusion.3
  114.0 2.9 fusion.18
  117.0 0.7 convolution_convert_fusion.2.terms_ref
  117.7 27.5 %sum_norm_gather.1 = (f32[128,1024]{1,0:T(8,128)S(1)}, bf16[1024,1024]{1,0:T(8,128)(2,1)S(1)}) custom-call(bf16[1024,1024]{1,0:T(8,128)(2,1)S(1)} %convolution_convert_fusion.2.terms_ref, bf16[128,1024]{1,0:T(8,128)(2,1)S(1)} %get-tuple-element.56.x_ref, f32[1,1024]{1,0:T(1,128)S(1)} %copy-done.15), custom_call_target="tpu_custom_call" | custom-call | tf_op jit(solution)/shard_map/sum_norm_gather/pallas_call | solution.py:613
  145.3 1.0 fusion.13
  146.3 1.9 multiply_convert_fusion
  148.1 1.7 convolution_convert_fusion.5
  149.8 0.9 convolution_convert_fusion.6
  150.8 2.9 convolution_convert_fusion.terms_ref
  153.6 1.9 convolution_convert_fusion.3.terms_ref
  155.5 29.4 %sum_back_gather.1 = (f32[128,1024]{1,0:T(8,128)S(1)}, f32[1,1024]{1,0:T(1,128)S(1)}, bf16[1024,1024]{1,0:T(8,128)(2,1)S(1)}) custom-call(bf16[1024,1024]{1,0:T(8,128)(2,1)S(1)} %convolution_convert_fusion.3.terms_ref, f32[128,1024]{1,0:T(8,128)S(1)} %get-tuple-element.58.stream_ref, f32[1,1024]{1,0:T(1,128)S(1)} %copy-done.15, ...), custom_call_target="tpu_custom_call" | custom-call | tf_op jit(solution)/shard_map/sum_back_gather/pallas_call | solution.py:613
  184.9 3.4 %multiply_reduce_fusion.8 = (f32[256]{0:T(256)S(1)}, f32[1024]{0:T(1024)S(1)}, bf16[1024,256]{1,0:T(8,128)(2,1)}, f32[1024,256]{1,0:T(8,128)S(1)}) fusion(f32[1024,256]{1,0:T(8,128)S(1)} %get-tuple-element.55, f32[1024]{0:T(1024)S(1)} %fusion.40, f32[1024,896]{1,0:T(8,128)} %fusion.53, f32[256]{0:T(256)S(1)} %bitcast.112, ...), kind=kOutput, calls=%fused_computation.45 | convolution fusion | flops 542112512 | bytes 6301696 | tf_op jit(solution)/shard_map/dot_general | solution.py:653
  188.4 2.6 add_add_fusion.do_ref
  191.0 0.8 convolution_convert_fusion.7
  191.8 1.8 pad_maximum_fusion
  193.6 4.7 %copy.62 = bf16[1024,1312]{1,0:T(8,128)(2,1)} copy(bf16[1024,1312]{0,1:T(8,128)(2,1)} %pad_maximum_fusion) | data formatting | bytes 5373952
  198.3 3.8 %pad.105.clone = bf16[1024,1408]{1,0:T(8,128)(2,1)} pad(bf16[1024,1312]{1,0:T(8,128)(2,1)} %copy.62, bf16[]{:T(256)} %constant.12.clone.1), padding=0_0x0_96 | pad | bytes 5570562 | tf_op jit(solution)/shard_map/jit(_pad)/pad | solution.py:657
  202.1 43.9 %delta_backward.1 = (f32[1024,128]{1,0:T(8,128)S(1)}, f32[1024,128]{1,0:T(8,128)S(1)}, f32[1024,256]{1,0:T(8,128)}, f32[1024,128]{1,0:T(8,128)S(1)}, f32[1024,12...) custom-call(f32[1024,128]{1,0:T(8,128)S(1)} %get-tuple-element.169.q_ref, ...), custom_call_target="tpu_custom_call" | custom-call | tf_op jit(solution)/shard_map/delta_backward/pallas_call | solution.py:613
  246.0 0.8 copy-done.8
  247.5 0.6 multiply_reduce_fusion.17
  248.8 0.7 maximum_bitcast_fusion
  249.5 1.2 multiply_reduce_fusion.11
  250.8 1.7 multiply_reduce_fusion.14
  252.5 0.8 add_add_fusion.2
  254.4 4.0 %multiply_reduce_fusion.3 = (f32[256]{0:T(256)S(1)}, f32[256]{0:T(256)S(1)}, f32[256]{0:T(256)S(1)}, f32[256]{0:T(256)S(1)}, f32[256]{0:T(256)S(1)}, /*index=5*/...) fusion(f32[1024,896]{1,0:T(8,128)} %fusion.53, ...), kind=kLoop, calls=%fused_computation.40 | loop fusion | flops 9172992 | bytes 10493952 | tf_op jit(solution)/shard_map/transpose(jvp())/reduce_sum | solution.py:631
  258.5 2.2 convert_reduce_fusion
  260.7 0.6 slice_bitcast_fusion.1
  261.3 0.7 slice_bitcast_fusion
  262.1 0.9 reshape.212
  263.2 2.0 fusion.20
  265.2 1.0 copy.53
  266.2 1.1 mul.521
  267.3 1.2 add_convert_fusion
  270.0 1.2 copy-done.19
  271.3 2.4 convolution_convert_fusion.4
  273.7 3.7 %convolution_convert_fusion.1.terms_ref = bf16[1024,1024]{1,0:T(8,128)(2,1)} fusion(bf16[1024,896]{1,0:T(8,128)(2,1)S(1)} %bitcast.94, bf16[1024,128]{1,0:T(8,128)(2,1)S(1)} %add_convert_fusion, bf16[1024,256]{1,0:T(8,128)(2,1)S(1)} %copy-done.36, bf16[1024,256]{1,0:T(8,128)(2,1)S(1)} %fusion.8, bf16[1024,256]{1,0:T(8,128)(2,1)S(1)} %fusion.9), kind=kOutput, calls=%fused_computation.4 | convolution fusion | flops 1887436800 | bytes 5767168 | tf_op jit(solution)/shard_map/dot_general | solution.py:653
  277.5 43.2 %exit_exchange.1 = (bf16[128,1024]{1,0:T(8,128)(2,1)S(1)}, bf16[128,1024]{1,0:T(8,128)(2,1)S(1)}, bf16[16,64,896]{2,1,0:T(8,128)(2,1)S(1)}, f32[48,128]{1,0:T(8,128)S(1)}) custom-call(bf16[1024,1024]{1,0:T(8,128)(2,1)} %convolution_convert_fusion.1.terms_ref, bf16[128,1024]{1,0:T(8,128)(2,1)S(1)} %get-tuple-element.56.x_ref, f32[1,1024]{1,0:T(1,128)S(1)} %copy-done.17, ...), custom_call_target="tpu_custom_call" | custom-call | tf_op jit(solution)/shard_map/exit_exchange/pallas_call | solution.py:613
  320.7 0.6 slice.198
  321.2 0.6 fusion.51
  321.8 0.6 fusion.50
  322.7 0.6 copy.57
  323.4 0.7 broadcast_in_dim.98
  324.1 0.7 broadcast_in_dim.97
  324.8 0.8 bitcast_convert_fusion.1
  325.6 0.8 bitcast_convert_fusion
  (103 shorter events, 5.7 us)
Async XLA Ops:
  6.3 1.0 copy-start.13
  7.3 0.9 copy-start.14
  8.2 0.7 copy-start.16
  44.4 1.2 copy-start.20
  45.6 7.0 %copy-start.18 = (bf16[1024,1024]{1,0:T(8,128)(2,1)}, bf16[1024,1024]{1,0:T(8,128)(2,1)S(1)}, u32[]{:S(2)}) copy-start(bf16[1024,1024]{1,0:T(8,128)(2,1)S(1)} %get-tuple-element.44) | copy-start | bytes 6291460
  60.0 2.4 copy-start.24
  60.0 2.4 copy-start.26
  62.3 1.0 copy-start.22
  63.3 47.9 %copy-start.34 = (f32[1,256]{1,0:T(1,128)S(1)}, f32[1,256]{1,0:T(1,128)}, u32[]{:S(2)}) copy-start(f32[1,256]{1,0:T(1,128)} %param.24) | copy-start | bytes 3076
  110.9 6.0 %copy-start.1 = (f32[1024,256]{1,0:T(8,128)}, f32[1024,256]{1,0:T(8,128)S(1)}, u32[]{:S(2)}) copy-start(f32[1024,256]{1,0:T(8,128)S(1)} %get-tuple-element.49.u_ref) | copy-start | bytes 3145732
  111.0 6.0 %copy-start.2 = (f32[1024,128]{1,0:T(8,128)}, f32[1024,128]{1,0:T(8,128)S(1)}, u32[]{:S(2)}) copy-start(f32[1024,128]{1,0:T(8,128)S(1)} %get-tuple-element.48.t_ref) | copy-start | bytes 1572868
  111.0 6.0 %copy-start.4 = (f32[1024,128]{1,0:T(8,128)}, f32[1024,128]{1,0:T(8,128)S(1)}, u32[]{:S(2)}) copy-start(f32[1024,128]{1,0:T(8,128)S(1)} %get-tuple-element.51.f_ref) | copy-start | bytes 1572868
  111.0 6.0 %copy-start.6 = (f32[1024,128]{1,0:T(8,128)}, f32[1024,128]{1,0:T(8,128)S(1)}, u32[]{:S(2)}) copy-start(f32[1024,128]{1,0:T(8,128)S(1)} %get-tuple-element.52.w_ref) | copy-start | bytes 1572868
  111.0 3.1 copy-start.33
  117.0 0.8 copy-start.15
  145.3 10.2 %copy-start = (f32[128,1024]{1,0:T(8,128)}, f32[128,1024]{1,0:T(8,128)S(1)}, u32[]{:S(2)}) copy-start(f32[128,1024]{1,0:T(8,128)S(1)} %get-tuple-element.58.stream_ref) | copy-start | bytes 1572868
  148.1 1.7 copy-start.35
  184.9 3.5 %copy-start.9 = (f32[128,1024]{1,0:T(8,128)}, f32[128,1024]{1,0:T(8,128)S(1)}, u32[]{:S(2)}) copy-start(f32[128,1024]{1,0:T(8,128)S(1)} %get-tuple-element.65.grad_ref) | copy-start | bytes 1572868
  198.3 3.8 %copy-start.3 = (f32[1024,128]{1,0:T(8,128)S(1)}, f32[1024,128]{1,0:T(8,128)}, u32[]{:S(2)}) copy-start(f32[1024,128]{1,0:T(8,128)} %copy-done.2) | copy-start | bytes 1572868
  198.3 3.8 %copy-start.5 = (f32[1024,128]{1,0:T(8,128)S(1)}, f32[1024,128]{1,0:T(8,128)}, u32[]{:S(2)}) copy-start(f32[1024,128]{1,0:T(8,128)} %copy-done.4) | copy-start | bytes 1572868
  198.3 3.8 %copy-start.7 = (f32[1024,128]{1,0:T(8,128)S(1)}, f32[1024,128]{1,0:T(8,128)}, u32[]{:S(2)}) copy-start(f32[1024,128]{1,0:T(8,128)} %copy-done.6) | copy-start | bytes 1572868
  246.0 0.8 copy-start.8
  246.8 0.7 copy-start.11
  246.8 5.7 %copy-start.23 = (f32[1024,256]{1,0:T(8,128)S(1)}, f32[1024,256]{1,0:T(8,128)}, u32[]{:S(2)}) copy-start(f32[1024,256]{1,0:T(8,128)} %copy-done.22) | copy-start | bytes 3145732
  250.8 2.6 copy-start.29
  250.8 2.6 copy-start.32
  252.5 1.3 copy-start.25
  252.5 1.6 copy-start.27
  252.5 1.9 copy-start.28
  260.7 5.5 %copy-start.31 = (f32[1024,1]{1,0:T(8,128)S(1)}, f32[1024,1]{1,0:T(8,128)}, u32[]{:S(2)}) copy-start(f32[1024,1]{1,0:T(8,128)} %copy.54) | copy-start | bytes 12292
  265.2 3.4 %copy-start.30 = (f32[1024,256]{1,0:T(8,128)S(1)}, f32[1024,256]{1,0:T(8,128)}, u32[]{:S(2)}) copy-start(f32[1024,256]{1,0:T(8,128)} %get-tuple-element.141) | copy-start | bytes 3145732
  269.6 1.6 copy-start.19
  269.6 1.7 copy-start.36
  271.3 2.4 copy-start.21
  273.7 3.7 %copy-start.10 = (f32[128,1024]{1,0:T(8,128)S(1)}, f32[128,1024]{1,0:T(8,128)}, u32[]{:S(2)}) copy-start(f32[128,1024]{1,0:T(8,128)} %copy-done.9) | copy-start | bytes 1572868
  273.7 3.7 %copy-start.12 = (bf16[128,1024]{1,0:T(8,128)(2,1)S(1)}, bf16[128,1024]{1,0:T(8,128)(2,1)}, u32[]{:S(2)}) copy-start(bf16[128,1024]{1,0:T(8,128)(2,1)} %copy-done.11) | copy-start | bytes 786436
  273.7 3.7 %copy-start.17 = (f32[1,1024]{1,0:T(1,128)S(1)}, f32[1,1024]{1,0:T(1,128)}, u32[]{:S(2)}) copy-start(f32[1,1024]{1,0:T(1,128)} %gain_ref.7) | copy-start | bytes 12292
